TPU v7x, 32 devices: a whole 2x2x4 slice. The times are simulated.
32 devices in a mesh: seq: 16 (over z, y, core), blk: 2 (over x).
Axes of the slice: x: 2, y: 2, z: 4, core: 2. Of those that a mesh axis runs over, the one named last changes fastest.
Arguments:
- tokens: bfloat16 [32, 1024, 768], P('seq', 'blk'), may hold values from -6 to 6
- sent_lengths: int32 [32, 4], P('seq'), may hold values from 0 to 1024, as said below
- w_query: bfloat16 [768, 768], P('seq'), may hold values from -0.21875 to 0.21875
- w_key: bfloat16 [768, 768], P('seq'), may hold values from -0.21875 to 0.21875
- w_value: bfloat16 [768, 768], P('seq'), may hold values from -0.21875 to 0.21875
- w_out: bfloat16 [768, 768], P('seq'), may hold values from -1.75 to 1.75
- shared_a: bfloat16 [768, 1024], P('seq'), may hold values from -0.21875 to 0.21875
- shared_b: bfloat16 [1024, 768], P('seq'), may hold values from -0.1875 to 0.1875
- w_in: bfloat16 [768, 3072], P('seq'), may hold values from -0.21875 to 0.21875
- w_back: bfloat16 [3072, 768], P('seq'), may hold values from -0.109375 to 0.109375
- gain_one: float32 [768], replicated, may hold values from 0.5 to 1.5
- gain_two: float32 [768], replicated, may hold values from 0.5 to 1.5
- scale_dq: float32 [1024], replicated, may hold values from 0.5 to 2
- shift_bq: float32 [768], replicated, may hold values from -4 to 4
- scale_dv: float32 [1024], replicated, may hold values from 0.5 to 2
- shift_bv: float32 [768], replicated, may hold values from -4 to 4
- cotangent: bfloat16 [32, 1024, 768], P('seq', 'blk'), may hold values from -6 to 6
Outputs:
- layer_out: bfloat16 [32, 1024, 768], P('seq', 'blk')
- grad_tokens: bfloat16 [32, 1024, 768], P('seq', 'blk')
- grad_dq: float32 [1024], replicated
- grad_bq: float32 [768], replicated
- grad_dv: float32 [1024], replicated
- grad_bv: float32 [768], replicated
Inputs may be any that keep to these rules, and one draw needn't show every extreme that they name: `sent_lengths`: rows come in groups of 2 (the rows of one index of seq). In each group one row holds a single document of 1024 tokens and empty other slots. Every other row holds two to four sentences in order and then padding: the first two have 8 to 512 tokens each, the third and fourth 0 to 1024 // 2 (the fourth empty when the third is), and all together at most 1024 tokens.
All inputs are finite; a program needn't handle non-finite values.
Results may differ from a plain program's by a relative error of at most 0.024.
Values may be sent and summed in bfloat16 or wider, within the bound.
No kernel may reach another device: no remote copies, remote signals or barrier semaphores. Data moves between devices by JAX's collectives and lax.ppermute only.
A program may use at most 192 MiB of HBM per device.

v0:
```python
import functools

import jax
import jax.numpy as jnp
from jax import lax
from jax.experimental import pallas as pl
from jax.experimental.pallas import tpu as pltpu
from jax.sharding import PartitionSpec as P

HEADS = 12
HEAD_DIM = 64
bf16 = jnp.bfloat16
f32 = jnp.float32


LN2 = 0.6931471805599453
LOG2E = 1.4426950408889634
SEGS = 5
PARTS = 3
TILE = 256
STEP = 128

def dot_nt(a,b): return lax.dot_general(a,b,(((1,),(1,)),((),())),preferred_element_type=f32)
def dot_nn(a,b): return jnp.dot(a,b,preferred_element_type=f32)

def lane_row(test, wide, kind=f32):
    lane = lax.broadcasted_iota(jnp.int32, (1, wide), 1)
    return jnp.where(test(lane), 1.0, 0.0).astype(kind)

def part_rows(wide, start):
    return [lane_row(lambda l: l == start + n, wide) for n in range(PARTS)]

def spread(column, rows):
    top = column.astype(bf16).astype(f32)
    return (top*rows[0] + (column-top)*rows[1]).astype(bf16)

def cross_ones(wide, hd):
    a = lax.broadcasted_iota(jnp.int32, (wide, wide), 0) < hd
    b = lax.broadcasted_iota(jnp.int32, (wide, wide), 1) < hd
    return jnp.where(a != b, 1.0, 0.0).astype(bf16)

def side_rows(wide, hd):
    return [lane_row(lambda l: l < hd, wide, bf16), lane_row(lambda l: l >= hd, wide, bf16)]

def bounds_of(lens, row):
    bounds = [lens[row, 0]]
    for n in range(1, SEGS-1):
        bounds.append(bounds[-1] + lens[row, n])
    return bounds

def key_span(bounds, i, span):
    low = 0
    for bound in bounds:
        low = jnp.where(bound <= i*TILE, bound, low)
    high = span
    for bound in reversed(bounds):
        high = jnp.where(bound > i*TILE + TILE-1, bound, high)
    begin = lax.div(low, STEP)
    count = lax.div(high - begin*STEP + TILE-1, TILE)
    return jnp.minimum(begin, lax.div(span - count*TILE, STEP)), count

def marks(bounds, span, wide, hd, side):
    place = lax.broadcasted_iota(jnp.int32, (span, wide), 0)
    lane = lax.broadcasted_iota(jnp.int32, (span, wide), 1) - (hd if side == 0 else 0)
    lane = jnp.where((lane >= 0) & (lane < hd), lane, hd)
    seg = jnp.zeros((span, wide), jnp.int32)
    for bound in bounds:
        seg = seg + jnp.where(place >= bound, 1, 0)
    asked = jnp.where((lane < SEGS) & (lane != seg), 1.0, 0.0).astype(bf16)
    held = jnp.where(lane == seg, -1e30, jnp.where((lane >= SEGS) & (lane < SEGS+PARTS), 1.0, 0.0)).astype(bf16)
    return asked, held

def by_half(mine, work):
    for n in range(2):
        @pl.when(mine == n)
        def _():
            work(n)

def query_tiles(bounds, span, work, broad):
    tiles = span//TILE
    fewest = tiles
    for i in range(tiles):
        fewest = jnp.minimum(fewest, key_span(bounds, i, span)[1])
    @pl.when(fewest == tiles)
    def _():
        def one(i, carry):
            work(pl.ds(pl.multiple_of(i*broad, broad), broad), slice(0, span))
            return carry
        lax.fori_loop(0, span//broad, one, 0)
    @pl.when(fewest < tiles)
    def _():
        def one(i, carry):
            rows = pl.ds(pl.multiple_of(i*TILE, TILE), TILE)
            begin, count = key_span(bounds, i, span)
            start = pl.multiple_of(begin*STEP, STEP)
            for n in range(1, tiles+1):
                @pl.when(count == n)
                def _():
                    work(rows, pl.ds(start, n*TILE) if n < tiles else slice(0, span))
            return carry
        lax.fori_loop(0, tiles, one, 0)

def attend_kernel(spot, lens, xo_ref, xp_ref, own_ref, par_ref, qa_ref, qf, kf, ka, va, og, outs, *, hd, row):
    half = xo_ref.shape[0]
    bounds = bounds_of(lens, row)
    span = 2*half
    wide = 2*hd
    sides = side_rows(wide, hd)
    swap = cross_ones(wide, hd)
    first = lax.broadcasted_iota(jnp.int32, (span, wide), 1) < hd
    start = [hd+SEGS, SEGS]
    parts = [part_rows(wide, start[s]) for s in range(2)]
    @pl.when(pl.program_id(0) == 0)
    def _():
        for s in range(2):
            qf[s], kf[s] = marks(bounds, span, wide, hd, s)
    longest = None
    for x_ref in (xo_ref, xp_ref):
        kp = x_ref[:, wide:2*wide]
        norms = jnp.max(dot_nn(kp*kp, swap), axis=0, keepdims=True)
        longest = norms if longest is None else jnp.maximum(longest, norms)
    def place(n):
        for x_ref, at in ((xo_ref, n), (xp_ref, 1-n)):
            rows = slice(at*half, (at+1)*half)
            qp = x_ref[:, 0:wide]
            kp = x_ref[:, wide:2*wide]
            vp = x_ref[:, 2*wide:3*wide]
            top = jnp.sqrt(dot_nn(qp*qp, swap) * longest) * 1.02
            for s in range(2):
                qa_ref[s, rows, :] = qp*sides[s] + (qf[s, rows, :] - (top*parts[s][0]).astype(bf16))
                ka[s, rows, :] = kp*sides[s] + kf[s, rows, :]
                va[s, rows, :] = vp*sides[s] + sides[1-s]
    by_half(spot[0], place)
    def weigh(rows, keys):
        for s in range(2):
            w = jnp.exp2(dot_nt(qa_ref[s, rows, :], ka[s, keys, :])).astype(bf16)
            og[s, rows, :] = dot_nn(w, va[s, keys, :])
    query_tiles(bounds, span, weigh, 512)
    @pl.when(jnp.logical_not(jnp.min(jnp.where(first, og[1], og[0])) > 2.0**-80))
    def _():
        def exact_tile(i, carry):
            rows = pl.ds(pl.multiple_of(i*TILE, TILE), TILE)
            for s in range(2):
                plain = qa_ref[s, rows, :] * (1.0 - parts[s][0]).astype(bf16)
                m = jnp.max(dot_nt(plain, ka[s]), axis=1, keepdims=True)
                qa_ref[s, rows, :] = plain - (jnp.broadcast_to(m, (TILE, wide))*parts[s][0]).astype(bf16)
            weigh(rows, slice(0, span))
            return carry
        lax.fori_loop(0, span//TILE, exact_tile, 0)
    total = jnp.where(first, og[1], og[0])
    outs[...] = (jnp.where(first, og[0], og[1]) / pltpu.roll(total, hd, 1)).astype(bf16)
    lse = -jnp.log2(total)
    for s in range(2):
        qa_ref[s] = qa_ref[s] + spread(lse, parts[s][1:])
    def leave(n):
        own_ref[...] = outs[n*half:(n+1)*half, :]
        par_ref[...] = outs[(1-n)*half:(2-n)*half, :]
    by_half(spot[0], leave)

def attend(row, spot, lens, qkv, heads, hd):
    count = lens.shape[0]
    half = qkv.shape[0]//(2*count); span = 2*half; mine = heads*hd; wide = 2*hd
    col = lambda p, s, l: (0, p)
    return pl.pallas_call(
        functools.partial(attend_kernel, hd=hd, row=row),
        grid_spec=pltpu.PrefetchScalarGridSpec(
            num_scalar_prefetch=2, grid=(heads//2,),
            in_specs=[pl.BlockSpec((half, 3*wide), lambda p, s, l: (row, p)), pl.BlockSpec((half, 3*wide), lambda p, s, l: (count+row, p))],
            out_specs=[
                pl.BlockSpec((half, wide), col),
                pl.BlockSpec((half, wide), col),
                pl.BlockSpec((2, span, wide), lambda p, s, l: (p, 0, 0)),
            ],
            scratch_shapes=[
                pltpu.VMEM((2, span, wide), bf16),
                pltpu.VMEM((2, span, wide), bf16),
                pltpu.VMEM((2, span, wide), bf16),
                pltpu.VMEM((2, span, wide), bf16),
                pltpu.VMEM((2, span, wide), f32),
                pltpu.VMEM((span, wide), bf16),
            ]),
        out_shape=[
            jax.ShapeDtypeStruct((half, mine), bf16),
            jax.ShapeDtypeStruct((half, mine), bf16),
            jax.ShapeDtypeStruct((heads, span, wide), bf16),
        ],
        compiler_params=pltpu.CompilerParams(vmem_limit_bytes=32<<20),
        cost_estimate=pl.CostEstimate(flops=16*span*span*mine, bytes_accessed=span*mine*12, transcendentals=span*span*heads),
    )(spot, lens, qkv, qkv)

def attend_back_kernel(spot, lens, xo_ref, xp_ref, co_ref, cp_ref, go_ref, gp_ref, qa_ref, *refs, hd, row):
    out_ref, kf, ka, va, ga, kt, kacc, vacc, qacc = refs[-9:]
    half = xo_ref.shape[0]
    bounds = bounds_of(lens, row)
    span = 2*half
    wide = 2*hd
    sides = side_rows(wide, hd)
    low = [lane_row(lambda l: (l >= hd) & (l < hd+PARTS), wide, bf16), lane_row(lambda l: l < PARTS, wide, bf16)]
    parts = [part_rows(wide, hd), part_rows(wide, 0)]
    swap = cross_ones(wide, hd)
    first = lax.broadcasted_iota(jnp.int32, (half, wide), 1) < hd
    @pl.when(pl.program_id(0) == 0)
    def _():
        for s in range(2):
            kf[s] = marks(bounds, span, wide, hd, s)[1]
    def place(n):
        for x_ref, c_ref, g_ref, at in ((xo_ref, co_ref, go_ref, n), (xp_ref, cp_ref, gp_ref, 1-n)):
            rows = slice(at*half, (at+1)*half)
            kp = x_ref[:, wide:2*wide]
            vp = x_ref[:, 2*wide:3*wide]
            gp = g_ref[...]
            kt[:, rows] = kp.T
            prod = gp.astype(f32) * c_ref[...].astype(f32)
            top = prod.astype(bf16)
            delta = dot_nn(top, swap) + dot_nn((prod - top.astype(f32)).astype(bf16), swap)
            for s in range(2):
                ka[s, rows, :] = kp*sides[s] + kf[s, rows, :]
                va[s, rows, :] = vp*sides[s] + low[s]
                ga[s, rows, :] = gp*sides[s] + spread(-delta, parts[s])
    by_half(spot[0], place)
    kacc[...] = jnp.zeros_like(kacc)
    vacc[...] = jnp.zeros_like(vacc)
    def work(rows, keys):
        for s in range(2):
            qq = qa_ref[s, rows, :]
            gg = ga[s, rows, :]
            probs = jnp.exp2(dot_nt(ka[s, keys, :], qq))
            slope = (probs * dot_nt(va[s, keys, :], gg)).astype(bf16)
            vacc[s, keys, :] += dot_nn(probs.astype(bf16), gg)
            kacc[s, keys, :] += dot_nn(slope, qq)
            qacc[s*hd:(s+1)*hd, rows] = dot_nn(kt[s*hd:(s+1)*hd, keys], slope)
    query_tiles(bounds, span, work, 2*TILE)
    def leave(n):
        for part, at in ((0, n), (1, 1-n)):
            rows = slice(at*half, (at+1)*half)
            out_ref[part, :, 0:wide] = (qacc[:, rows].T * LN2).astype(bf16)
            out_ref[part, :, wide:2*wide] = (jnp.where(first, kacc[0, rows, :], kacc[1, rows, :]) * LN2).astype(bf16)
            out_ref[part, :, 2*wide:3*wide] = jnp.where(first, vacc[0, rows, :], vacc[1, rows, :]).astype(bf16)
    by_half(spot[0], leave)

def attend_back(row, spot, lens, qkv, ctx_own, ctx_par, g_own, g_par, qa, before, heads, hd):
    count = lens.shape[0]
    half = qkv.shape[0]//(2*count); span = 2*half; mine = heads*hd; wide = 2*hd
    col = lambda p, s, l: (0, p)
    at_row = lambda p, s, l: (row, p)
    return pl.pallas_call(
        functools.partial(attend_back_kernel, hd=hd, row=row),
        grid_spec=pltpu.PrefetchScalarGridSpec(
            num_scalar_prefetch=2, grid=(heads//2,),
            in_specs=[pl.BlockSpec((half, 3*wide), at_row), pl.BlockSpec((half, 3*wide), lambda p, s, l: (count+row, p))] + [pl.BlockSpec((half, wide), col)]*4
            + [pl.BlockSpec((2, span, wide), lambda p, s, l: (p, 0, 0))] + [pl.BlockSpec(memory_space=pl.ANY)]*len(before),
            out_specs=pl.BlockSpec((2, half, 3*wide), lambda p, s, l: (0, row, p)),
            scratch_shapes=[
                pltpu.VMEM((2, span, wide), bf16),
                pltpu.VMEM((2, span, wide), bf16),
                pltpu.VMEM((2, span, wide), bf16),
                pltpu.VMEM((2, span, wide), bf16),
                pltpu.VMEM((wide, span), bf16),
                pltpu.VMEM((2, span, wide), f32),
                pltpu.VMEM((2, span, wide), f32),
                pltpu.VMEM((wide, span), f32),
            ]),
        out_shape=jax.ShapeDtypeStruct((2, count*half, 3*mine), bf16),
        input_output_aliases={9+n: n for n in range(len(before))},
        compiler_params=pltpu.CompilerParams(vmem_limit_bytes=(50 if row + 1 < count else 44)<<20),
        cost_estimate=pl.CostEstimate(flops=40*span*span*mine, bytes_accessed=span*mine*20, transcendentals=span*span*heads),
    )(spot, lens, qkv, qkv, ctx_own, ctx_par, g_own, g_par, qa, *before)


def pack_kernel(place, a_ref, q_ref, k_ref, v_ref, b_ref, out_ref, in_ref, back_ref, *refs, wide):
    vectors, (first_ref, second_ref, vecs) = refs[:-3], refs[-3:]
    vecs[...] = jnp.zeros_like(vecs)
    for n, ref in enumerate(vectors):
        vecs[n : n + 1, : ref.shape[0]] = ref[...].reshape(1, ref.shape[0])
    lead = a_ref.shape[0]
    width = out_ref.shape[1]
    row = 0
    pieces = [a_ref[:, at : at + wide] for at in range(0, a_ref.shape[1], wide)]
    for at in range(0, q_ref.shape[1], wide):
        pieces += [ref[:, at : at + wide] for ref in (q_ref, k_ref, v_ref)]
    pieces += [b_ref[:, at : at + wide] for at in range(0, b_ref.shape[1], wide)]
    for piece in pieces:
        first_ref[row : row + piece.shape[0], :] = piece
        row += piece.shape[0]
    row = 0
    pieces = [out_ref[...]]
    pieces += [in_ref[:, at : at + width] for at in range(0, in_ref.shape[1], width)]
    pieces += [back_ref[...]]
    for piece in pieces:
        second_ref[row : row + piece.shape[0], :] = piece
        row += piece.shape[0]


def packed(place, shared_a, w_query, w_key, w_value, shared_b, w_out, w_in, w_back, vectors, part, wide):
    lead, rank = shared_a.shape
    width = w_out.shape[1]
    rows = lead * (rank + 3 * part) // wide + shared_b.shape[0] * part // wide
    whole = lambda array: pl.BlockSpec(array.shape, lambda i, s: (0, 0))
    half = lambda array: pl.BlockSpec((array.shape[0], part), lambda i, s: (0, s[0]))
    total = lead + lead * w_in.shape[1] // width + w_back.shape[0]
    return pl.pallas_call(
        functools.partial(pack_kernel, wide=wide),
        grid_spec=pltpu.PrefetchScalarGridSpec(
            num_scalar_prefetch=1,
            grid=(1,),
            in_specs=[whole(shared_a), half(w_query), half(w_key), half(w_value), half(shared_b), whole(w_out), whole(w_in), whole(w_back)]
            + [pl.BlockSpec(vector.shape, lambda i, s: (0,)) for vector in vectors],
            out_specs=[pl.BlockSpec((rows, wide), lambda i, s: (0, 0)), pl.BlockSpec((total, width), lambda i, s: (0, 0)), pl.BlockSpec((8, rank), lambda i, s: (0, 0))],
        ),
        out_shape=[jax.ShapeDtypeStruct((rows, wide), bf16), jax.ShapeDtypeStruct((total, width), bf16), jax.ShapeDtypeStruct((8, rank), f32)],
        compiler_params=pltpu.CompilerParams(vmem_limit_bytes=60 << 20),
    )(place, shared_a, w_query, w_key, w_value, shared_b, w_out, w_in, w_back, *vectors)


def bent(vecs, at, side, part):
    row = vecs[at : at + 1, : 2 * part]
    return jnp.where(side == 0, row[:, :part], row[:, part:])


def merge_kernel(spot, *refs, shards, rank, part, wide):
    quads = refs[:4]
    vecs, down, lift, weights, merged, mixed = refs[4:]
    each = quads[0].shape[0] // 4
    lead = down.shape[1]
    deep = lift.shape[1]
    pairs = part // wide
    for j in range(shards):
        at = spot[1] ^ j
        piece = quads[j % 4]
        row = each * (j // 4)
        for n in range(rank // wide):
            down[at, :, n * wide : (n + 1) * wide] = piece[row : row + lead, :]
            row += lead
        for n in range(3 * pairs):
            mixed[at, :, n * wide : (n + 1) * wide] = piece[row : row + lead, :]
            row += lead
        for n in range(pairs):
            lift[at, :, n * wide : (n + 1) * wide] = piece[row : row + deep, :]
            row += deep
    low = down[...].reshape(shards * lead, rank)
    high = lift[...].reshape(shards * deep, part)
    delta_q = dot_nn(low * vecs[0:1, :].astype(bf16), high)
    merged[:, :part] = delta_q.astype(bf16)
    delta_q = delta_q * bent(vecs, 2, spot[0], part)
    delta_v = dot_nn(low * vecs[1:2, :].astype(bf16), high)
    merged[:, part:] = delta_v.astype(bf16)
    delta_v = delta_v * bent(vecs, 3, spot[0], part)
    for n in range(pairs):
        cols = slice(n * wide, (n + 1) * wide)
        base = 3 * n * wide
        get = lambda s: mixed[:, :, base + s * wide : base + (s + 1) * wide].reshape(shards * lead, wide)
        weights[:, base : base + wide] = ((get(0).astype(f32) + delta_q[:, cols]) * (0.125 * LOG2E)).astype(bf16)
        weights[:, base + wide : base + 2 * wide] = get(1)
        weights[:, base + 2 * wide : base + 3 * wide] = (get(2).astype(f32) + delta_v[:, cols]).astype(bf16)


def merge(spot, quads, vecs, shards, lead, deep, rank, part, wide):
    width = shards * lead
    whole = lambda shape: pl.BlockSpec(shape, lambda i, s: (0,) * len(shape))
    return pl.pallas_call(
        functools.partial(merge_kernel, shards=shards, rank=rank, part=part, wide=wide),
        grid_spec=pltpu.PrefetchScalarGridSpec(
            num_scalar_prefetch=1,
            grid=(1,),
            in_specs=[whole(quads[0].shape)] * 4 + [whole(vecs.shape)],
            out_specs=[whole((shards, lead, rank)), whole((shards, deep, part)), whole((width, 3 * part)), whole((width, 2 * part))],
            scratch_shapes=[pltpu.VMEM((shards, lead, 3 * part), bf16)],
        ),
        out_shape=[
            jax.ShapeDtypeStruct((shards, lead, rank), bf16),
            jax.ShapeDtypeStruct((shards, deep, part), bf16),
            jax.ShapeDtypeStruct((width, 3 * part), bf16),
            jax.ShapeDtypeStruct((width, 2 * part), bf16),
        ],
        compiler_params=pltpu.CompilerParams(vmem_limit_bytes=40 << 20),
        cost_estimate=pl.CostEstimate(flops=40 * width * rank * part, bytes_accessed=1 << 20, transcendentals=0),
    )(spot, *quads, vecs)


def flipped(block, mask):
    count = lax.axis_size("seq")
    return lax.ppermute(block, "seq", [(i, i ^ mask) for i in range(count)])


def far_piece(piece):
    count = lax.axis_size("seq")
    pairs = [(2 * i + b, 2 * (i ^ (8 + 4 * b)) + b) for i in range(count) for b in range(2)]
    return lax.ppermute(piece, ("seq", "blk"), pairs)


def spread_square(block):
    across = flipped(block, 2)
    return [block, flipped(block, 1), across, flipped(across, 1)]


def trained_kernel(
    spot, turned_ref, grad_ref, vecs, merged_hbm, down_hbm, lift_hbm, out_ref, moment, merged_ref, down_ref, lift_ref, sems,
    *, wide
):
    held = ((merged_hbm, merged_ref), (down_hbm, down_ref), (lift_hbm, lift_ref))
    lead = down_ref.shape[1]
    width = down_ref.shape[0] * lead
    rank = down_ref.shape[2]
    part = lift_ref.shape[2]
    pairs = part // wide
    picked = [grad_ref[:, (3 * n + s) * wide : (3 * n + s + 1) * wide] for s in (0, 2) for n in range(pairs)]
    added = dot_nn(turned_ref[...], jnp.concatenate(picked, axis=1))
    @pl.when(pl.program_id(0) == 0)
    def _():
        for n, (source, target) in enumerate(held):
            pltpu.make_async_copy(source, target, sems.at[n]).start()
        moment[...] = added
    @pl.when(pl.program_id(0) > 0)
    def _():
        moment[...] += added
    @pl.when(pl.program_id(0) == pl.num_programs(0) - 1)
    def _():
        for n, (source, target) in enumerate(held):
            pltpu.make_async_copy(source, target, sems.at[n]).wait()
        down = down_ref[...].reshape(width, rank).astype(f32)
        lift = lift_ref[...].reshape(rank, part)
        out_ref[...] = jnp.zeros_like(out_ref)
        base = 0
        for s, coef in ((0, 0.125 * LOG2E), (1, 1.0)):
            cols = slice(s * part, (s + 1) * part)
            shift = jnp.sum(merged_ref[:, cols].astype(f32) * moment[:, cols], axis=0, keepdims=True) * coef
            bend = bent(vecs, 2 + s, spot[0], part) * coef
            bent_moment = (moment[:, cols] * bend).astype(bf16)
            scale = jnp.sum(down * dot_nt(bent_moment, lift), axis=0, keepdims=True)
            for n in range(rank // wide):
                out_ref[base + n : base + n + 1, :] = scale[:, n * wide : (n + 1) * wide]
            base += rank // wide
            for n in range(pairs):
                out_ref[pl.ds(base + pairs * spot[0] + n, 1), :] = shift[:, n * wide : (n + 1) * wide]
            base += 2 * pairs


def trained(spot, turned, grads, merged, down, lift, vecs, wide):
    rank, part = down.shape[2], lift.shape[2]
    width, total = turned.shape
    step = total // 2
    whole = lambda array: pl.BlockSpec(array.shape, lambda i, s: (0,) * array.ndim)
    rows = 2 * (rank + 2 * part) // wide
    return pl.pallas_call(
        functools.partial(trained_kernel, wide=wide),
        grid_spec=pltpu.PrefetchScalarGridSpec(
            num_scalar_prefetch=1,
            grid=(2,),
            in_specs=[
                pl.BlockSpec((width, step), lambda i, s: (0, i)),
                pl.BlockSpec((step, grads.shape[1]), lambda i, s: (i, 0)),
            ]
            + [whole(vecs)] + [pl.BlockSpec(memory_space=pl.ANY)] * 3,
            out_specs=pl.BlockSpec((rows, wide), lambda i, s: (0, 0)),
            scratch_shapes=[pltpu.VMEM((width, 2 * part), f32)]
            + [pltpu.VMEM(array.shape, bf16) for array in (merged, down, lift)] + [pltpu.SemaphoreType.DMA((3,))],
        ),
        out_shape=jax.ShapeDtypeStruct((rows, wide), f32),
        compiler_params=pltpu.CompilerParams(vmem_limit_bytes=60 << 20),
        cost_estimate=pl.CostEstimate(flops=8 * width * total * part, bytes_accessed=12 << 20, transcendentals=0),
    )(spot, turned, grads, vecs, merged, down, lift)


def finish_kernel(turned_ref, w_ref, grad_ref, *refs):
    sent, out_ref = refs[:-1], refs[-1]
    held = grad_ref[...].astype(f32) + dot_nt(turned_ref[...], w_ref[...])
    for n, ref in enumerate(sent):
        @pl.when(pl.program_id(0) == n)
        def _():
            out_ref[...] = (held + ref[...].astype(f32)).astype(bf16)


def finish(grad_one, turned, weights, sent):
    count, span, width = grad_one.shape
    at_row = pl.BlockSpec((None, span, width), lambda i: (i, 0, 0))
    cols = turned.shape[2]
    return pl.pallas_call(
        finish_kernel,
        grid=(count,),
        in_specs=[
            pl.BlockSpec((None, span, cols), lambda i: (0, i, 0)),
            pl.BlockSpec((width, cols), lambda i: (0, 0)),
            at_row,
        ]
        + [pl.BlockSpec((span, width), lambda i: (0, 0))] * count,
        out_specs=at_row,
        out_shape=jax.ShapeDtypeStruct((count, span, width), bf16),
        compiler_params=pltpu.CompilerParams(vmem_limit_bytes=48 << 20),
    )(turned, weights, grad_one, *sent)


def centred(hidden):
    off = hidden - jnp.mean(hidden, axis=-1, keepdims=True)
    scale = lax.rsqrt(jnp.mean(off*off, axis=-1, keepdims=True) + 1e-05)
    return off*scale, scale

def norm_back(grad, unit, scale):
    inner = jnp.mean(grad*unit, axis=-1, keepdims=True)
    return scale*(grad - jnp.mean(grad, axis=-1, keepdims=True) - unit*inner)

def gelu_pair(x):
    size = jnp.abs(x)
    base = 1.0 + size*(0.3275911*0.7071067811865476)
    t = pl.reciprocal(base, approx=True)
    t = t*(2.0 - base*t)
    bell = jnp.exp2(x*x*(-0.7213475204444817))
    tail = t*(0.127414796 + t*(-0.142248368 + t*(0.7107068705 + t*(-0.7265760135 + t*0.5307027145))))*bell
    below = jnp.where(x < 0, tail, 1.0 - tail)
    return x*below, below + x*(bell*0.3989422804014327)

def ffn_kernel(spot, co_hbm, cr_hbm, x_hbm, cot_hbm, g1_ref, g2_ref, *refs, shards, cuts, row):
    pieces = refs[:shards]
    out_ref, grad_ref, own_ref, send_ref, co_ref, cr_ref, x_ref, cot_ref, wo, wi, wb, slopes, acts, sems = refs[-14:]
    width = x_ref.shape[1]
    lead = wo.shape[1]
    back = wb.shape[1]
    per = shards//cuts
    mine = spot[0]
    seat = spot[1]
    groups = [0, 4, 8 + 4*mine, 12 - 4*mine]
    ats = [seat ^ (groups[j//per] + j%per) for j in range(shards)]
    def bring(source, target, n):
        pltpu.make_async_copy(source, target, sems.at[n]).start()
    def arrived(held, n):
        pltpu.make_async_copy(held, held, sems.at[n]).wait()
    bring(co_hbm, co_ref, 1+2*cuts)
    bring(cr_hbm, cr_ref, 2+2*cuts)
    bring(x_hbm.at[row], x_ref, 3+2*cuts)
    for j in range(shards):
        bring(pieces[j].at[0:lead, :], wo.at[ats[j]], 0)
    for g in range(cuts):
        block = lax.shift_right_logical(seat ^ groups[g], 2)
        start = pl.multiple_of(lead*(1+block), 16)
        for j in range(shards):
            bring(pieces[j].at[pl.ds(start, lead), :], wi.at[g, ats[j]], 1+g)
        for j in range(g*per, (g+1)*per):
            bring(pieces[j].at[lead*(1+cuts):lead*(1+cuts)+back, :], wb.at[g*per + (ats[j] & (per-1))], 1+cuts+g)
    bring(cot_hbm.at[row], cot_ref, 4+2*cuts)
    part = shards//2
    half = width//2
    def out_rows(who):
        return wo[pl.ds(pl.multiple_of(who*part, part), part)].reshape(half, width)
    def w_in(j): return wi[j].reshape(width, width)
    def w_back(j): return wb[j*per:(j+1)*per].reshape(per*back, width)
    arrived(co_ref, 1+2*cuts)
    arrived(cr_ref, 2+2*cuts)
    arrived(x_ref, 3+2*cuts)
    arrived(wo, 0)
    resid = x_ref[...].astype(f32) + dot_nn(co_ref[...], out_rows(mine)) + dot_nn(cr_ref[...], out_rows(1-mine))
    unit_one, scale_one = centred(resid)
    gain_one = g1_ref[...].reshape(1, width)
    gain_two = g2_ref[...].reshape(1, width)
    normed = unit_one*gain_one
    low = normed.astype(bf16)
    total = normed
    for j in range(cuts):
        arrived(wi.at[j], 1+j)
        arrived(wb.at[j*per:(j+1)*per], 1+cuts+j)
    for j in range(cuts):
        for at in range(0, width, 256):
            for top in range(0, x_ref.shape[0], 256):
                act, slope = gelu_pair(dot_nn(low[top:top+256], wi[j, :, :, at:at+256].reshape(width, 256)))
                acts[top:top+256, at:at+256] = act.astype(bf16)
                slopes[j, top:top+256, at:at+256] = slope.astype(bf16)
        total = total + dot_nn(acts[...], w_back(j))
    unit_two, scale_two = centred(total)
    out_ref[...] = (unit_two*gain_two).astype(bf16)
    arrived(cot_ref, 4+2*cuts)
    grad_two = norm_back(cot_ref[...].astype(f32)*gain_two, unit_two, scale_two)
    low_two = grad_two.astype(bf16)
    grad = grad_two
    for j in range(cuts):
        pre_grad = (dot_nt(low_two, w_back(j))*slopes[j].astype(f32)).astype(bf16)
        grad = grad + dot_nt(pre_grad, w_in(j))
    grad_one = norm_back(grad*gain_one, unit_one, scale_one)
    low_one = grad_one.astype(bf16)
    grad_ref[...] = low_one
    send_ref[...] = dot_nt(low_one, out_rows(1-mine)).astype(bf16)
    own_ref[...] = dot_nt(low_one, out_rows(mine)).astype(bf16)

def ffn(row, spot, ctx_own, ctx_recv, x, cot, gain_one, gain_two, pieces, before, cuts):
    count, span, width = x.shape
    shards = len(pieces)
    lead = width//shards
    back = cuts*width//shards
    whole = lambda shape: pl.BlockSpec(shape, lambda i, s: (0,)*len(shape))
    at_row = pl.BlockSpec((None, span, width), lambda i, s: (row, 0, 0))
    anywhere = pl.BlockSpec(memory_space=pl.ANY)
    return pl.pallas_call(
        functools.partial(ffn_kernel, shards=shards, cuts=cuts, row=row),
        grid_spec=pltpu.PrefetchScalarGridSpec(
            num_scalar_prefetch=1, grid=(1,),
            in_specs=[anywhere]*4 + [whole((width,))]*2 + [anywhere]*(shards+len(before)),
            out_specs=[at_row, at_row, whole((span, width//2)), whole((span, width//2))],
            scratch_shapes=[
                pltpu.VMEM((span, width//2), bf16),
                pltpu.VMEM((span, width//2), bf16),
                pltpu.VMEM((span, width), bf16),
                pltpu.VMEM((span, width), bf16),
                pltpu.VMEM((shards, lead, width), bf16),
                pltpu.VMEM((cuts, shards, lead, width), bf16),
                pltpu.VMEM((shards, back, width), bf16),
                pltpu.VMEM((cuts, span, width), bf16),
                pltpu.VMEM((span, width), bf16),
                pltpu.SemaphoreType.DMA((5+2*cuts,)),
            ]),
        out_shape=[
            jax.ShapeDtypeStruct((count, span, width), bf16),
            jax.ShapeDtypeStruct((count, span, width), bf16),
            jax.ShapeDtypeStruct((span, width//2), bf16),
            jax.ShapeDtypeStruct((span, width//2), bf16),
        ],
        input_output_aliases={7+shards+n: n for n in range(len(before))},
        compiler_params=pltpu.CompilerParams(vmem_limit_bytes=56<<20),
        cost_estimate=pl.CostEstimate(flops=8*span*width*width*(2+4*cuts), bytes_accessed=2*(2+2*cuts)*width*width, transcendentals=2*span*width*cuts),
    )(spot, ctx_own, ctx_recv, x, cot, gain_one, gain_two, *pieces, *before)


def shifted(shard, axis, by):
    count = lax.axis_size(axis)
    return lax.ppermute(shard, axis, [(i, (i + by) % count) for i in range(count)])


def layer_norm(hidden, gain):
    centre = hidden - jnp.mean(hidden, axis=-1, keepdims=True)
    spread = jnp.mean(centre * centre, axis=-1, keepdims=True)
    return centre * lax.rsqrt(spread + 1e-05) * gain


def exact_gelu(values):
    return jax.nn.gelu(values, approximate=False)


def segment_ids(lengths, total):
    place = jnp.arange(total, dtype=jnp.int32)[None, :]
    bounds = jnp.cumsum(lengths, axis=1)
    counted = jnp.zeros((lengths.shape[0], total), jnp.int32)
    for column in range(lengths.shape[1]):
        counted = counted + (place >= bounds[:, column : column + 1]).astype(jnp.int32)
    return counted


def dot_plain(left, right):
    return jnp.dot(left, right, preferred_element_type=jnp.float32)


def dot_trans(left, right):
    return lax.dot_general(
        left, right, (((1,), (1,)), ((), ())), preferred_element_type=jnp.float32
    )


def block_grads(query_h, out_grad, lse_rows, delta_rows, key_h, value_h, allowed):
    scores = (
        jnp.einsum("rqhd,rkhd->rqhk", query_h, key_h, preferred_element_type=jnp.float32) * 0.125
    )
    probs = jnp.where(allowed, jnp.exp(scores - lse_rows[..., None]), 0.0)
    value_grad = jnp.einsum(
        "rqhk,rqhd->rkhd", probs.astype(jnp.bfloat16), out_grad, preferred_element_type=jnp.float32
    )
    prob_grad = jnp.einsum("rqhd,rkhd->rqhk", out_grad, value_h, preferred_element_type=jnp.float32)
    score_grad = (probs * (prob_grad - delta_rows[..., None])).astype(jnp.bfloat16)
    query_grad = (
        jnp.einsum("rqhk,rkhd->rqhd", score_grad, key_h, preferred_element_type=jnp.float32) * 0.125
    )
    key_grad = (
        jnp.einsum("rqhk,rqhd->rkhd", score_grad, query_h, preferred_element_type=jnp.float32)
        * 0.125
    )
    return (query_grad, key_grad, value_grad)


def body_any(
    tokens,
    sent_lengths,
    w_query,
    w_key,
    w_value,
    w_out,
    shared_a,
    shared_b,
    w_in,
    w_back,
    gain_one,
    gain_two,
    scale_dq,
    shift_bq,
    scale_dv,
    shift_bv,
    cotangent,
):
    row_count, span, width = tokens.shape
    head_count = HEADS
    head_size = HEAD_DIM
    blocks = lax.axis_size("blk")
    my_block = lax.axis_index("blk")
    token_count = row_count * span
    token_rows = tokens.reshape(token_count, width)
    seg_full = segment_ids(sent_lengths, span * blocks)
    seg_mine = lax.dynamic_slice_in_dim(seg_full, my_block * span, span, 1)
    w_queries, w_keys, w_values, proj_a, proj_b = (
        lax.all_gather(w_query, "seq", axis=0, tiled=True),
        lax.all_gather(w_key, "seq", axis=0, tiled=True),
        lax.all_gather(w_value, "seq", axis=0, tiled=True),
        lax.all_gather(shared_a, "seq", axis=0, tiled=True),
        lax.all_gather(shared_b, "seq", axis=0, tiled=True),
    )
    projected = dot_plain(token_rows, proj_a).astype(jnp.bfloat16)
    proj_float = projected.astype(jnp.float32)
    lift_q = (proj_float * scale_dq).astype(jnp.bfloat16)
    lift_v = (proj_float * scale_dv).astype(jnp.bfloat16)
    extra_q = dot_plain(lift_q, proj_b)
    extra_v = dot_plain(lift_v, proj_b)
    queries = (dot_plain(token_rows, w_queries) + shift_bq * extra_q).astype(jnp.bfloat16)
    key_rows = dot_plain(token_rows, w_keys).astype(jnp.bfloat16)
    value_rows = (dot_plain(token_rows, w_values) + shift_bv * extra_v).astype(jnp.bfloat16)
    shape4 = (row_count, span, head_count, head_size)
    query_h = queries.reshape(shape4)
    key_h = key_rows.reshape(shape4)
    value_h = value_rows.reshape(shape4)
    start_best = jnp.full((row_count, span, head_count), -1e30, jnp.float32)
    best = start_best
    key_piece = lax.all_gather(key_rows.reshape(row_count, span, width), "blk", axis=1, tiled=True)
    value_piece = lax.all_gather(
        value_rows.reshape(row_count, span, width), "blk", axis=1, tiled=True
    )
    length = key_piece.shape[1]
    key_part = key_piece.reshape(row_count, length, head_count, head_size)
    value_part = value_piece.reshape(row_count, length, head_count, head_size)
    seg_keys = seg_full
    allowed = (seg_mine[:, :, None] == seg_keys[:, None, :])[:, :, None, :]
    scores = (
        jnp.einsum("rqhd,rkhd->rqhk", query_h, key_part, preferred_element_type=jnp.float32) * 0.125
    )
    scores = jnp.where(allowed, scores, -1e30)
    new_best = jnp.maximum(best, jnp.max(scores, axis=-1))
    weight = jnp.where(allowed, jnp.exp(scores - new_best[..., None]), 0.0)
    total = jnp.sum(weight, axis=-1)
    accum = jnp.einsum(
        "rqhk,rkhd->rqhd",
        weight.astype(jnp.bfloat16),
        value_part,
        preferred_element_type=jnp.float32,
    )
    best, total, accum = (new_best, total, accum)
    log_total = best + jnp.log(total)
    context = accum / total[..., None]
    context_b = context.reshape(token_count, width).astype(jnp.bfloat16)
    w_outs, w_ins, w_backs = (
        lax.all_gather(w_out, "seq", axis=0, tiled=True),
        lax.all_gather(w_in, "seq", axis=0, tiled=True),
        lax.all_gather(w_back, "seq", axis=0, tiled=True),
    )

    def norm_first(hidden):
        return layer_norm(hidden, gain_one)

    def norm_second(hidden):
        return layer_norm(hidden, gain_two)

    resid_one = token_rows.astype(jnp.float32) + dot_plain(context_b, w_outs)
    normed_one, norm_one_pull = jax.vjp(norm_first, resid_one)
    pre_act = dot_plain(normed_one.astype(jnp.bfloat16), w_ins)
    act_float, gelu_pull = jax.vjp(exact_gelu, pre_act)
    ffn_part = dot_plain(act_float.astype(jnp.bfloat16), w_backs)
    normed_two, norm_two_pull = jax.vjp(norm_second, normed_one + ffn_part)
    layer_out = normed_two.astype(jnp.bfloat16).reshape(row_count, span, width)
    w_outs, w_ins, w_backs = (
        lax.all_gather(w_out, "seq", axis=0, tiled=True),
        lax.all_gather(w_in, "seq", axis=0, tiled=True),
        lax.all_gather(w_back, "seq", axis=0, tiled=True),
    )
    (grad_two,) = norm_two_pull(cotangent.reshape(token_count, width).astype(jnp.float32))
    act_grad = dot_trans(grad_two.astype(jnp.bfloat16), w_backs)
    (pre_grad,) = gelu_pull(act_grad)
    normed_grad = grad_two + dot_trans(pre_grad.astype(jnp.bfloat16), w_ins)
    (grad_one,) = norm_one_pull(normed_grad)
    context_grad = dot_trans(grad_one.astype(jnp.bfloat16), w_outs).astype(jnp.bfloat16)
    out_grad = context_grad.reshape(shape4)
    delta_rows = jnp.sum(out_grad.astype(jnp.float32) * context, axis=-1)
    zero_grads = jnp.zeros(shape4, jnp.float32)

    def key_step(step, carry):
        key_cur, value_cur, query_acc, key_acc, value_acc = carry
        source = (my_block - step) % blocks
        seg_keys = lax.dynamic_slice_in_dim(seg_full, source * span, span, 1)
        allowed = (seg_mine[:, :, None] == seg_keys[:, None, :])[:, :, None, :]
        q_part, k_part, v_part = block_grads(
            query_h, out_grad, log_total, delta_rows, key_cur, value_cur, allowed
        )
        key_acc, value_acc = (
            shifted((key_acc + k_part).astype(jnp.bfloat16), "blk", 1).astype(jnp.float32),
            shifted((value_acc + v_part).astype(jnp.bfloat16), "blk", 1).astype(jnp.float32),
        )
        key_cur, value_cur = shifted((key_cur, value_cur), "blk", 1)
        return (key_cur, value_cur, query_acc + q_part, key_acc, value_acc)

    looped = lax.fori_loop(
        0, blocks, key_step, (key_h, value_h, zero_grads, zero_grads, zero_grads)
    )
    query_acc, key_acc, value_acc = (looped[2], looped[3], looped[4])
    query_grad = query_acc.reshape(token_count, width).astype(jnp.bfloat16)
    key_grad = key_acc.reshape(token_count, width).astype(jnp.bfloat16)
    value_grad = value_acc.reshape(token_count, width).astype(jnp.bfloat16)
    w_queries, w_keys, w_values, proj_a, proj_b = (
        lax.all_gather(w_query, "seq", axis=0, tiled=True),
        lax.all_gather(w_key, "seq", axis=0, tiled=True),
        lax.all_gather(w_value, "seq", axis=0, tiled=True),
        lax.all_gather(shared_a, "seq", axis=0, tiled=True),
        lax.all_gather(shared_b, "seq", axis=0, tiled=True),
    )
    query_float = query_grad.astype(jnp.float32)
    value_float = value_grad.astype(jnp.float32)
    part_bq = jnp.sum(query_float * extra_q, axis=0)
    part_bv = jnp.sum(value_float * extra_v, axis=0)
    lift_q_grad = dot_trans((query_float * shift_bq).astype(jnp.bfloat16), proj_b)
    lift_v_grad = dot_trans((value_float * shift_bv).astype(jnp.bfloat16), proj_b)
    part_dq = jnp.sum(lift_q_grad * proj_float, axis=0)
    part_dv = jnp.sum(lift_v_grad * proj_float, axis=0)
    proj_grad = (lift_q_grad * scale_dq + lift_v_grad * scale_dv).astype(jnp.bfloat16)
    token_grad = (
        grad_one
        + dot_trans(query_grad, w_queries)
        + dot_trans(key_grad, w_keys)
        + dot_trans(value_grad, w_values)
        + dot_trans(proj_grad, proj_a)
    )
    grad_dq, grad_bq, grad_dv, grad_bv = lax.psum(
        (part_dq, part_bq, part_dv, part_bv), ("seq", "blk")
    )
    return (
        layer_out,
        token_grad.astype(jnp.bfloat16).reshape(row_count, span, width),
        grad_dq,
        grad_bq,
        grad_dv,
        grad_bv,
    )


def swapped(block):
    return lax.ppermute(block, "blk", [(0, 1), (1, 0)])


def body_two(
    tokens,
    sent_lengths,
    w_query,
    w_key,
    w_value,
    w_out,
    shared_a,
    shared_b,
    w_in,
    w_back,
    gain_one,
    gain_two,
    scale_dq,
    shift_bq,
    scale_dv,
    shift_bv,
    cotangent,
):
    row_count, span, width = tokens.shape
    shards = lax.axis_size("seq")
    heads = HEADS // 2
    part = heads * HEAD_DIM
    wide = 2 * HEAD_DIM
    lead, rank = shared_a.shape
    deep = shared_b.shape[0]
    cuts = w_in.shape[1] // width
    rows = range(row_count)
    spot = jnp.stack([lax.axis_index("blk"), lax.axis_index("seq")]).astype(jnp.int32)

    first, second, vecs = packed(
        spot, shared_a, w_query, w_key, w_value, shared_b, w_out, w_in, w_back,
        (scale_dq, scale_dv, shift_bq, shift_bv), part, wide,
    )
    tie = lax.optimization_barrier

    def core(block):
        return flipped(block, 1)

    other = swapped(tokens)
    lines = [flipped(first, 4), flipped(first, 8), flipped(first, 12)]
    second_over = flipped(second, 2)
    lines, second_over, second = tie((lines, second_over, second))
    quad = jnp.concatenate([first] + lines, axis=0)
    quad_over = flipped(quad, 2)
    quad_core = core(quad)
    far = far_piece(second)
    near = flipped(second, 4)
    both = jnp.concatenate([tokens, other], axis=0).reshape(2 * row_count * span, width)
    turned = both.T
    quad_over, quad_core, far, near, both, turned = tie((quad_over, quad_core, far, near, both, turned))
    down, lift, weights, merged = merge(
        spot, (quad, quad_core, quad_over, core(quad_over)), vecs, shards, lead, deep, rank, part, wide
    )
    qkv = dot_nn(both, weights).astype(bf16)
    near_core, far_core = core(near), core(far)
    qkv, second, second_over, far, near, near_core, far_core = tie(
        (qkv, second, second_over, far, near, near_core, far_core)
    )
    last = swapped(far)
    far_over = flipped(far, 2)
    near_over = flipped(second_over, 4)
    second_core, second_over_core = core(second), core(second_over)
    seen = [attend(0, spot, sent_lengths, qkv, heads, HEAD_DIM)]
    seen[0], last, far_over, near_over, second_core, second_over_core, qkv, near, far = tie(
        (seen[0], last, far_over, near_over, second_core, second_over_core, qkv, near, far)
    )
    ctx_recv = [swapped(seen[0][1])]
    last_over = flipped(last, 2)
    near_over_core, far_over_core, last_core = core(near_over), core(far_over), core(last)
    seen.append(attend(1, spot, sent_lengths, qkv, heads, HEAD_DIM))
    seen[1], ctx_recv[0], last_over, near_over_core, far_over_core, last_core = tie(
        (seen[1], ctx_recv[0], last_over, near_over_core, far_over_core, last_core)
    )
    ctx_recv.append(swapped(seen[1][1]))
    pack = [second, second_core, second_over, second_over_core, near, near_core, near_over, near_over_core]
    pack += [far, far_core, far_over, far_over_core, last, last_core, last_over, core(last_over)]
    fed = []
    for row in rows:
        before = fed[-1][:2] if fed else []
        fed.append(
            ffn(row, spot, seen[row][0], ctx_recv[row], tokens, cotangent, gain_one, gain_two, pack, before, cuts)
        )
    layer_out, grad_one = fed[-1][:2]
    grad_recv = [swapped(fed[row][3]) for row in rows]
    sent = []
    grads = []
    for row in rows:
        whole = attend_back(
            row, spot, sent_lengths, qkv, seen[row][0], seen[row][1],
            fed[row][2], grad_recv[row], seen[row][2], grads, heads, HEAD_DIM,
        )
        partial = dot_nt(whole[1, row * span : (row + 1) * span], weights).astype(bf16)
        if sent:
            whole, partial, sent[-1] = tie((whole, partial, sent[-1]))
        whole, partial = tie((whole, partial))
        grads = [whole]
        sent.append(swapped(partial))
    flat = trained(
        spot, turned, whole.reshape(2 * row_count * span, 3 * part), merged, down, lift, vecs, wide
    )
    flat = flat + core(flat)
    flat = flat + flipped(flat, 2)
    level, far_levels = flipped(flat, 4), flipped(flat, 8) + flipped(flat, 12)
    level, sent[-1] = tie((level, sent[-1]))
    flat = (flat + level) + far_levels
    flat = (flat + swapped(flat)).reshape(-1)
    token_grad = finish(grad_one, whole, weights, sent)
    return (
        layer_out,
        token_grad,
        flat[:rank],
        flat[rank : rank + width],
        flat[rank + width : 2 * rank + width],
        flat[2 * rank + width :],
    )


def solution(mesh):
    return jax.shard_map(
        body_two if mesh.shape["blk"] == 2 and mesh.shape["seq"] == 16 else body_any,
        mesh=mesh,
        in_specs=(
            P("seq", "blk", None),
            P("seq", None),
            P("seq", None),
            P("seq", None),
            P("seq", None),
            P("seq", None),
            P("seq", None),
            P("seq", None),
            P("seq", None),
            P("seq", None),
            P(),
            P(),
            P(),
            P(),
            P(),
            P(),
            P("seq", "blk", None),
        ),
        out_specs=(P("seq", "blk", None), P("seq", "blk", None), P(), P(), P(), P()),
        check_vma=False,
    )
```

profile of v0, /device:TPU:0, one launch (start us, length us, event | category | flops | bytes accessed | tf_op | source)
XLA Modules:
  0.0 272.5 jit_solution(5831974876264105816)
XLA Ops:
  1.2 2.9 %shard_map.208 = (bf16[1008,128]{1,0:T(8,128)(2,1)}, bf16[432,768]{1,0:T(8,128)(2,1)}, f32[8,1024]{1,0:T(8,128)}) custom-call(s32[2]{0:T(128)} %pad_add_fusion.place.spot, bf16[48,1024]{1,0:T(8,128)(2,1)} %a_ref.1, bf16[48,768]{1,0:T(8,128)(2,1)} %q_ref.1, bf16[48,768]{1,0:T(8,128)(2,1)} %k_ref.1, bf16[48,768]{1,0:T(8,128)(2,1)} %v_ref.1, ...), custom_call_target="tpu_custom_call" | custom-call | tf_op jit(solution)/shard_map/pallas_call | solution.py:301
  4.1 3.0 %collective-permute-start.3 = (bf16[432,768]{1,0:T(8,128)(2,1)}, bf16[432,768]{1,0:T(8,128)(2,1)S(1)}, u32[]{:S(2)}, u32[]{:S(2)}) collective-permute-start(bf16[432,768]{1,0:T(8,128)(2,1)} %get-tuple-element.93.refs_0_), channel_id=1, source_target_pairs={{0,4},{2,6},{4,0},{6,2},{8,12},{10,14},{12,8},{14,10},{16,20},{18,... | collective-permute-start | bytes 1990664 | tf_op jit(solution)/shard_map/ppermute | solution.py:382
  8.6 3.6 %collective-permute-start.2 = (bf16[1008,128]{1,0:T(8,128)(2,1)}, bf16[1008,128]{1,0:T(8,128)(2,1)S(1)}, u32[]{:S(2)}, u32[]{:S(2)}) collective-permute-start(bf16[1008,128]{1,0:T(8,128)(2,1)} %get-tuple-element.73), channel_id=1, source_target_pairs={{0,24},{2,26},{4,28},{6,30},{8,16},{10,18},{12,20},{14,22},{16,8},... | collective-permute-start | bytes 774152 | tf_op jit(solution)/shard_map/ppermute | solution.py:382
  14.0 5.9 %collective-permute-done.2 = bf16[1008,128]{1,0:T(8,128)(2,1)S(1)} collective-permute-done((bf16[1008,128]{1,0:T(8,128)(2,1)}, bf16[1008,128]{1,0:T(8,128)(2,1)S(1)}, u32[]{:S(2)}, u32[]{:S(2)}) %collective-permute-start.2) | collective-permute-done | bytes 258080 | tf_op jit(solution)/shard_map/ppermute | solution.py:382
  19.9 13.9 %collective-permute-done.1 = bf16[1008,128]{1,0:T(8,128)(2,1)S(1)} collective-permute-done((bf16[1008,128]{1,0:T(8,128)(2,1)}, bf16[1008,128]{1,0:T(8,128)(2,1)S(1)}, u32[]{:S(2)}, u32[]{:S(2)}) %collective-permute-start.1) | collective-permute-done | bytes 258080 | tf_op jit(solution)/shard_map/ppermute | solution.py:382
  34.7 3.0 %collective-permute-start.6 = (bf16[432,768]{1,0:T(8,128)(2,1)}, bf16[432,768]{1,0:T(8,128)(2,1)}, u32[]{:S(2)}, u32[]{:S(2)}) collective-permute-start(bf16[432,768]{1,0:T(8,128)(2,1)} %get-tuple-element.93.refs_0_), channel_id=1, source_target_pairs={{0,16},{1,25},{2,18},{3,27},{4,20},{5,29},{6,22},{7,31},{8,24},{9,... | collective-permute-start | bytes 1990664 | tf_op jit(solution)/shard_map/ppermute | solution.py:388
  37.7 5.5 %collective-permute-done.8 = bf16[2,512,768]{2,1,0:T(8,128)(2,1)S(1)} collective-permute-done((bf16[2,512,768]{2,1,0:T(8,128)(2,1)}, bf16[2,512,768]{2,1,0:T(8,128)(2,1)S(1)}, u32[]{:S(2)}, u32[]{:S(2)}) %collective-permute-start.8) | collective-permute-done | bytes 1572896 | tf_op jit(solution)/shard_map/ppermute | solution.py:842
  45.1 4.8 %copy.27 = bf16[2048,768]{0,1:T(8,128)(2,1)} copy(bf16[2048,768]{1,0:T(8,128)(2,1)} %bitcast.24) | data formatting | bytes 6291456 | tf_op jit(solution)/shard_map/reshape | solution.py:893
  49.9 16.0 %collective-permute-done.7.refs_4_ = bf16[432,768]{1,0:T(8,128)(2,1)} collective-permute-done((bf16[432,768]{1,0:T(8,128)(2,1)}, bf16[432,768]{1,0:T(8,128)(2,1)}, u32[]{:S(2)}, u32[]{:S(2)}) %collective-permute-start.7) | collective-permute-done | bytes 663584 | tf_op jit(solution)/shard_map/ppermute | solution.py:382
  71.1 3.1 %shard_map.209 = (bf16[16,48,1024]{2,1,0:T(8,128)(2,1)S(1)}, bf16[16,64,384]{2,1,0:T(8,128)(2,1)S(1)}, bf16[768,1152]{1,0:T(8,128)(2,1)S(1)}, bf16[768,768]{1,0:T(8,128)(2,1)S(1)}) custom-call(s32[2]{0:T(128)S(1)} %copy-done.3, bf16[4032,128]{1,0:T(8,128)(2,1)S(1)} %constant_dynamic-update-slice_fusion.refs_0_, ...), custom_call_target="tpu_custom_call" | custom-call | flops 12079595520 | bytes 1048576 | tf_op jit(solution)/shard_map/pallas_call | solution.py:360
  76.2 4.6 %convolution_convert_fusion.xo_ref.xp_ref = bf16[2048,1152]{1,0:T(8,128)(2,1)S(1)} fusion(bf16[2048,768]{0,1:T(8,128)(2,1)S(1)} %copy-done.19, bf16[768,1152]{1,0:T(8,128)(2,1)S(1)} %get-tuple-element.83.w_ref), kind=kOutput, calls=%fused_computation | convolution fusion | flops 3626237952 | bytes 9633792 | tf_op jit(solution)/shard_map/dot_general | solution.py:24
  84.1 14.4 %shard_map.210 = (bf16[512,384]{1,0:T(8,128)(2,1)S(1)}, bf16[512,384]{1,0:T(8,128)(2,1)S(1)}, bf16[6,1024,128]{2,1,0:T(8,128)(2,1)S(1)}) custom-call(s32[2]{0:T(128)S(1)} %copy-done.3, s32[2,4]{1,0:T(2,128)S(1)} %copy-done.8, bf16[2048,1152]{1,0:T(8,128)(2,1)S(1)} %convolution_convert_fusion.xo_ref.xp_ref, ...), custom_call_target="tpu_custom_call" | custom-call | flops 6442450944 | bytes 4718592 | tf_op jit(solution)/shard_map/pallas_call | solution.py:164
  100.0 11.8 %collective-permute-start.19 = (bf16[432,768]{1,0:T(8,128)(2,1)S(1)}, bf16[432,768]{1,0:T(8,128)(2,1)S(1)}, u32[]{:S(2)}, u32[]{:S(2)}) collective-permute-start(bf16[432,768]{1,0:T(8,128)(2,1)S(1)} %collective-permute-done.14.refs_6_), channel_id=1, source_target_pairs={{0,2},{2,0},{4,6},{6,4},{8,10},{10,8},{12,14},{14,12},{16,18},{18,... | collective-permute-start | bytes 1990664 | tf_op jit(solution)/shard_map/ppermute | solution.py:382
  114.2 15.4 %shard_map.211 = (bf16[512,384]{1,0:T(8,128)(2,1)S(1)}, bf16[512,384]{1,0:T(8,128)(2,1)S(1)}, bf16[6,1024,128]{2,1,0:T(8,128)(2,1)S(1)}) custom-call(s32[2]{0:T(128)S(1)} %copy-done.3, s32[2,4]{1,0:T(2,128)S(1)} %copy-done.8, bf16[2048,1152]{1,0:T(8,128)(2,1)S(1)} %convolution_convert_fusion.xo_ref.xp_ref, ...), custom_call_target="tpu_custom_call" | custom-call | flops 6442450944 | bytes 4718592 | tf_op jit(solution)/shard_map/pallas_call | solution.py:164
  130.7 11.9 %collective-permute-start.23 = (bf16[432,768]{1,0:T(8,128)(2,1)S(1)}, bf16[432,768]{1,0:T(8,128)(2,1)}, u32[]{:S(2)}, u32[]{:S(2)}) collective-permute-start(bf16[432,768]{1,0:T(8,128)(2,1)S(1)} %collective-permute-done.18.refs_14_), channel_id=1, source_target_pairs={{0,2},{2,0},{4,6},{6,4},{8,10},{10,8},{12,14},{14,12},{16,18},{18,... | collective-permute-start | bytes 1990664 | tf_op jit(solution)/shard_map/ppermute | solution.py:382
  144.4 22.5 %shard_map.212 = (bf16[2,512,768]{2,1,0:T(8,128)(2,1)}, bf16[2,512,768]{2,1,0:T(8,128)(2,1)}, bf16[512,384]{1,0:T(8,128)(2,1)}, bf16[512,384]{1,0:T(8,128)(2,1)}) custom-call(s32[2]{0:T(128)} %pad_add_fusion.place.spot, bf16[512,384]{1,0:T(8,128)(2,1)} %copy-done.13, bf16[512,384]{1,0:T(8,128)(2,1)} %copy-done.35, bf16[2,512,768]{2,1,0:T(8,128)(2,1)} %x_hbm.3, ...), custom_call_target="tpu_custom_call" | custom-call | flops 43486543872 | bytes 11796480 | tf_op jit(solution)/shard_map/pallas_call | solution.py:589
  167.9 22.7 %shard_map.213 = (bf16[2,512,768]{2,1,0:T(8,128)(2,1)}, bf16[2,512,768]{2,1,0:T(8,128)(2,1)}, bf16[512,384]{1,0:T(8,128)(2,1)}, bf16[512,384]{1,0:T(8,128)(2,1)}) custom-call(s32[2]{0:T(128)} %pad_add_fusion.place.spot, bf16[512,384]{1,0:T(8,128)(2,1)} %copy-done.15, ...), custom_call_target="tpu_custom_call", output_to_operand_aliasing={{0}: (23, {}), {1}: (24, {})} | custom-call | flops 43486543872 | bytes 11796480 | tf_op jit(solution)/shard_map/pallas_call | solution.py:589
  191.9 17.9 %shard_map.214.refs_0_ = bf16[2,1024,1152]{2,1,0:T(8,128)(2,1)} custom-call(s32[2]{0:T(128)S(1)} %copy-done.4, s32[2,4]{1,0:T(2,128)S(1)} %copy-done.8, bf16[2048,1152]{1,0:T(8,128)(2,1)} %copy-done.10, bf16[2048,1152]{1,0:T(8,128)(2,1)} %copy-done.10, bf16[512,384]{1,0:T(8,128)(2,1)S(1)} %copy-done.14, bf16[512,384]{1,0:T(8,128)(2,1)S(1)} %get-tuple-element.99.cp_ref, ...), custom_call_target="tpu_custom_call" | custom-call | flops 16106127360 | bytes 7864320 | tf_op jit(solution)/shard_map/pallas_call | solution.py:246
  213.4 22.0 %shard_map.215.turned_ref = bf16[2,1024,1152]{2,1,0:T(8,128)(2,1)S(1)} custom-call(s32[2]{0:T(128)S(1)} %copy-done.4, s32[2,4]{1,0:T(2,128)S(1)} %copy-done.8, bf16[2048,1152]{1,0:T(8,128)(2,1)} %copy-done.10, bf16[2048,1152]{1,0:T(8,128)(2,1)} %copy-done.10, bf16[512,384]{1,0:T(8,128)(2,1)S(1)} %copy-done.16, ...), custom_call_target="tpu_custom_call", output_to_operand_aliasing={{}: (9, {})} | custom-call | flops 16106127360 | bytes 7864320 | tf_op jit(solution)/shard_map/pallas_call | solution.py:246
  239.0 8.8 %shard_map.216 = f32[28,128]{1,0:T(8,128)} custom-call(s32[2]{0:T(128)} %pad_add_fusion.place.spot, bf16[768,2048]{1,0:T(8,128)(2,1)} %bitcast.25, bf16[2048,1152]{1,0:T(8,128)(2,1)} %bitcast.23, f32[8,1024]{1,0:T(8,128)} %get-tuple-element.82.refs_4_.vecs, bf16[768,768]{1,0:T(8,128)(2,1)} %copy-done.11, bf16[16,48,1024]{2,1,0:T(8,128)(2,1)} %copy-done.9, ...), custom_call_target="tpu_custom_call" | custom-call | flops 4831838208 | bytes 12582912 | tf_op jit(solution)/shard_map/pallas_call | solution.py:444
  251.7 2.8 %collective-permute-start.28 = (f32[28,128]{1,0:T(8,128)S(1)}, f32[28,128]{1,0:T(8,128)S(1)}, u32[]{:S(2)}, u32[]{:S(2)}) collective-permute-start(f32[28,128]{1,0:T(8,128)S(1)} %add.18), channel_id=1, source_target_pairs={{0,4},{2,6},{4,0},{6,2},{8,12},{10,14},{12,8},{14,10},{16,20},{18,... | collective-permute-start | bytes 43016 | tf_op jit(solution)/shard_map/ppermute | solution.py:382
  256.2 5.0 %collective-permute-start.32 = (f32[28,128]{1,0:T(8,128)S(1)}, f32[28,128]{1,0:T(8,128)S(1)}, u32[]{:S(2)}, u32[]{:S(2)}) collective-permute-start(f32[28,128]{1,0:T(8,128)S(1)} %add.19), channel_id=1, source_target_pairs={{0,24},{2,26},{4,28},{6,30},{8,16},{10,18},{12,20},{14,22},{16,8},... | collective-permute-start | bytes 43016 | tf_op jit(solution)/shard_map/ppermute | solution.py:382
  263.1 2.7 %collective-permute-done.31 = f32[28,128]{1,0:T(8,128)S(1)} collective-permute-done((f32[28,128]{1,0:T(8,128)S(1)}, f32[28,128]{1,0:T(8,128)S(1)}, u32[]{:S(2)}, u32[]{:S(2)}) %collective-permute-start.31) | collective-permute-done | bytes 14368 | tf_op jit(solution)/shard_map/ppermute | solution.py:382
  266.0 5.1 %shard_map.217 = bf16[2,512,768]{2,1,0:T(8,128)(2,1)} custom-call(bf16[2,1024,1152]{2,1,0:T(8,128)(2,1)} %copy-done.1, bf16[768,1152]{1,0:T(8,128)(2,1)S(1)} %get-tuple-element.83.w_ref, bf16[2,512,768]{2,1,0:T(8,128)(2,1)S(1)} %copy-done.2, bf16[512,768]{1,0:T(8,128)(2,1)S(1)} %collective-permute-done.26.refs_0_, ...), custom_call_target="tpu_custom_call" | custom-call | tf_op jit(solution)/shard_map/pallas_call | solution.py:477
  (142 shorter events, 42.0 us)
Async XLA Ops:
  4.1 29.7 %collective-permute-start.3 = (bf16[432,768]{1,0:T(8,128)(2,1)}, bf16[432,768]{1,0:T(8,128)(2,1)S(1)}, u32[]{:S(2)}, u32[]{:S(2)}) collective-permute-start(bf16[432,768]{1,0:T(8,128)(2,1)} %get-tuple-element.93.refs_0_), channel_id=1, source_target_pairs={{0,4},{2,6},{4,0},{6,2},{8,12},{10,14},{12,8},{14,10},{16,20},{18,... | collective-permute-start | bytes 1990664 | tf_op jit(solution)/shard_map/ppermute | solution.py:382
  7.1 36.1 %collective-permute-start.8 = (bf16[2,512,768]{2,1,0:T(8,128)(2,1)}, bf16[2,512,768]{2,1,0:T(8,128)(2,1)S(1)}, u32[]{:S(2)}, u32[]{:S(2)}) collective-permute-start(bf16[2,512,768]{2,1,0:T(8,128)(2,1)} %x_hbm.3), channel_id=1, source_target_pairs={{0,1},{1,0},{2,3},{3,2},{4,5},{5,4},{6,7},{7,6},{8,9},{9,8},{10,11... | collective-permute-start | bytes 4718600 | tf_op jit(solution)/shard_map/ppermute | solution.py:842
  12.2 21.6 %collective-permute-start.1 = (bf16[1008,128]{1,0:T(8,128)(2,1)}, bf16[1008,128]{1,0:T(8,128)(2,1)S(1)}, u32[]{:S(2)}, u32[]{:S(2)}) collective-permute-start(bf16[1008,128]{1,0:T(8,128)(2,1)} %get-tuple-element.73), channel_id=1, source_target_pairs={{0,16},{2,18},{4,20},{6,22},{8,24},{10,26},{12,28},{14,30},{16,0},... | collective-permute-start | bytes 774152 | tf_op jit(solution)/shard_map/ppermute | solution.py:382
  12.2 21.6 %collective-permute-start = (bf16[1008,128]{1,0:T(8,128)(2,1)}, bf16[1008,128]{1,0:T(8,128)(2,1)S(1)}, u32[]{:S(2)}, u32[]{:S(2)}) collective-permute-start(bf16[1008,128]{1,0:T(8,128)(2,1)} %get-tuple-element.73), channel_id=1, source_target_pairs={{0,8},{2,10},{4,12},{6,14},{8,0},{10,2},{12,4},{14,6},{16,24},{18,... | collective-permute-start | bytes 774152 | tf_op jit(solution)/shard_map/ppermute | solution.py:382
  34.0 33.3 %collective-permute-start.5 = (bf16[4032,128]{1,0:T(8,128)(2,1)S(1)}, bf16[4032,128]{1,0:T(8,128)(2,1)S(1)}, u32[]{:S(2)}, u32[]{:S(2)}) collective-permute-start(bf16[4032,128]{1,0:T(8,128)(2,1)S(1)} %constant_dynamic-update-slice_fusion.refs_0_), channel_id=1, source_target_pairs={{0,2},{2,0},{4,6},{6,4},{8,10},{10,8},{12,14},{14,12},{16,18},{18,... | collective-permute-start | bytes 3096584 | tf_op jit(solution)/shard_map/ppermute | solution.py:382
  34.0 33.2 %collective-permute-start.4 = (bf16[4032,128]{1,0:T(8,128)(2,1)S(1)}, bf16[4032,128]{1,0:T(8,128)(2,1)S(1)}, u32[]{:S(2)}, u32[]{:S(2)}) collective-permute-start(bf16[4032,128]{1,0:T(8,128)(2,1)S(1)} %constant_dynamic-update-slice_fusion.refs_0_), channel_id=1, source_target_pairs={{0,4},{2,6},{4,0},{6,2},{8,12},{10,14},{12,8},{14,10},{16,20},{18,... | collective-permute-start | bytes 3096584 | tf_op jit(solution)/shard_map/ppermute | solution.py:382
  34.6 31.3 %collective-permute-start.7 = (bf16[432,768]{1,0:T(8,128)(2,1)}, bf16[432,768]{1,0:T(8,128)(2,1)}, u32[]{:S(2)}, u32[]{:S(2)}) collective-permute-start(bf16[432,768]{1,0:T(8,128)(2,1)} %get-tuple-element.93.refs_0_), channel_id=1, source_target_pairs={{0,8},{2,10},{4,12},{6,14},{8,0},{10,2},{12,4},{14,6},{16,24},{18,... | collective-permute-start | bytes 1990664 | tf_op jit(solution)/shard_map/ppermute | solution.py:382
  34.7 32.5 %collective-permute-start.6 = (bf16[432,768]{1,0:T(8,128)(2,1)}, bf16[432,768]{1,0:T(8,128)(2,1)}, u32[]{:S(2)}, u32[]{:S(2)}) collective-permute-start(bf16[432,768]{1,0:T(8,128)(2,1)} %get-tuple-element.93.refs_0_), channel_id=1, source_target_pairs={{0,16},{1,25},{2,18},{3,27},{4,20},{5,29},{6,22},{7,31},{8,24},{9,... | collective-permute-start | bytes 1990664 | tf_op jit(solution)/shard_map/ppermute | solution.py:388
  80.8 18.4 %collective-permute-start.13 = (bf16[432,768]{1,0:T(8,128)(2,1)}, bf16[432,768]{1,0:T(8,128)(2,1)S(1)}, u32[]{:S(2)}, u32[]{:S(2)}) collective-permute-start(bf16[432,768]{1,0:T(8,128)(2,1)} %collective-permute-done.6.refs_8_), channel_id=1, source_target_pairs={{0,4},{2,6},{4,0},{6,2},{8,12},{10,14},{12,8},{14,10},{16,20},{18,... | collective-permute-start | bytes 1990664 | tf_op jit(solution)/shard_map/ppermute | solution.py:382
  82.4 16.9 %collective-permute-start.12 = (bf16[432,768]{1,0:T(8,128)(2,1)}, bf16[432,768]{1,0:T(8,128)(2,1)S(1)}, u32[]{:S(2)}, u32[]{:S(2)}) collective-permute-start(bf16[432,768]{1,0:T(8,128)(2,1)} %collective-permute-done.6.refs_8_), channel_id=1, source_target_pairs={{0,1},{1,0},{2,3},{3,2},{4,5},{5,4},{6,7},{7,6},{8,9},{9,8},{10,11... | collective-permute-start | bytes 1990664 | tf_op jit(solution)/shard_map/ppermute | solution.py:842
  82.6 16.7 %collective-permute-start.15 = (bf16[432,768]{1,0:T(8,128)(2,1)S(1)}, bf16[432,768]{1,0:T(8,128)(2,1)S(1)}, u32[]{:S(2)}, u32[]{:S(2)}) collective-permute-start(bf16[432,768]{1,0:T(8,128)(2,1)S(1)} %copy-done.21), channel_id=1, source_target_pairs={{0,2},{2,0},{4,6},{6,4},{8,10},{10,8},{12,14},{14,12},{16,18},{18,... | collective-permute-start | bytes 1990664 | tf_op jit(solution)/shard_map/ppermute | solution.py:382
  82.6 16.7 %collective-permute-start.16 = (bf16[432,768]{1,0:T(8,128)(2,1)S(1)}, bf16[432,768]{1,0:T(8,128)(2,1)S(1)}, u32[]{:S(2)}, u32[]{:S(2)}) collective-permute-start(bf16[432,768]{1,0:T(8,128)(2,1)S(1)} %copy-done.23), channel_id=1, source_target_pairs={{0,2},{2,0},{4,6},{6,4},{8,10},{10,8},{12,14},{14,12},{16,18},{18,... | collective-permute-start | bytes 1990664 | tf_op jit(solution)/shard_map/ppermute | solution.py:382
  83.1 16.9 %collective-permute-start.14 = (bf16[432,768]{1,0:T(8,128)(2,1)S(1)}, bf16[432,768]{1,0:T(8,128)(2,1)S(1)}, u32[]{:S(2)}, u32[]{:S(2)}) collective-permute-start(bf16[432,768]{1,0:T(8,128)(2,1)S(1)} %copy-done.23), channel_id=1, source_target_pairs={{0,8},{2,10},{4,12},{6,14},{8,0},{10,2},{12,4},{14,6},{16,24},{18,... | collective-permute-start | bytes 1990664 | tf_op jit(solution)/shard_map/ppermute | solution.py:382
  100.0 29.6 %collective-permute-start.19 = (bf16[432,768]{1,0:T(8,128)(2,1)S(1)}, bf16[432,768]{1,0:T(8,128)(2,1)S(1)}, u32[]{:S(2)}, u32[]{:S(2)}) collective-permute-start(bf16[432,768]{1,0:T(8,128)(2,1)S(1)} %collective-permute-done.14.refs_6_), channel_id=1, source_target_pairs={{0,2},{2,0},{4,6},{6,4},{8,10},{10,8},{12,14},{14,12},{16,18},{18,... | collective-permute-start | bytes 1990664 | tf_op jit(solution)/shard_map/ppermute | solution.py:382
  111.8 17.9 %collective-permute-start.20 = (bf16[432,768]{1,0:T(8,128)(2,1)S(1)}, bf16[432,768]{1,0:T(8,128)(2,1)S(1)}, u32[]{:S(2)}, u32[]{:S(2)}) collective-permute-start(bf16[432,768]{1,0:T(8,128)(2,1)S(1)} %collective-permute-done.13.refs_10_), channel_id=1, source_target_pairs={{0,2},{2,0},{4,6},{6,4},{8,10},{10,8},{12,14},{14,12},{16,18},{18,... | collective-permute-start | bytes 1990664 | tf_op jit(solution)/shard_map/ppermute | solution.py:382
  111.9 17.8 %collective-permute-start.21 = (bf16[432,768]{1,0:T(8,128)(2,1)S(1)}, bf16[432,768]{1,0:T(8,128)(2,1)S(1)}, u32[]{:S(2)}, u32[]{:S(2)}) collective-permute-start(bf16[432,768]{1,0:T(8,128)(2,1)S(1)} %collective-permute-done.12.refs_12_), channel_id=1, source_target_pairs={{0,2},{2,0},{4,6},{6,4},{8,10},{10,8},{12,14},{14,12},{16,18},{18,... | collective-permute-start | bytes 1990664 | tf_op jit(solution)/shard_map/ppermute | solution.py:382
  112.3 17.4 %collective-permute-start.18 = (bf16[432,768]{1,0:T(8,128)(2,1)S(1)}, bf16[432,768]{1,0:T(8,128)(2,1)S(1)}, u32[]{:S(2)}, u32[]{:S(2)}) collective-permute-start(bf16[432,768]{1,0:T(8,128)(2,1)S(1)} %collective-permute-done.12.refs_12_), channel_id=1, source_target_pairs={{0,4},{2,6},{4,0},{6,2},{8,12},{10,14},{12,8},{14,10},{16,20},{18,... | collective-permute-start | bytes 1990664 | tf_op jit(solution)/shard_map/ppermute | solution.py:382
  113.1 16.6 %collective-permute-start.17 = (bf16[512,384]{1,0:T(8,128)(2,1)S(1)}, bf16[512,384]{1,0:T(8,128)(2,1)S(1)}, u32[]{:S(2)}, u32[]{:S(2)}) collective-permute-start(bf16[512,384]{1,0:T(8,128)(2,1)S(1)} %get-tuple-element.99.cp_ref), channel_id=1, source_target_pairs={{0,1},{1,0},{2,3},{3,2},{4,5},{5,4},{6,7},{7,6},{8,9},{9,8},{10,11... | collective-permute-start | bytes 1179656 | tf_op jit(solution)/shard_map/ppermute | solution.py:842
  130.7 13.8 %collective-permute-start.23 = (bf16[432,768]{1,0:T(8,128)(2,1)S(1)}, bf16[432,768]{1,0:T(8,128)(2,1)}, u32[]{:S(2)}, u32[]{:S(2)}) collective-permute-start(bf16[432,768]{1,0:T(8,128)(2,1)S(1)} %collective-permute-done.18.refs_14_), channel_id=1, source_target_pairs={{0,2},{2,0},{4,6},{6,4},{8,10},{10,8},{12,14},{14,12},{16,18},{18,... | collective-permute-start | bytes 1990664 | tf_op jit(solution)/shard_map/ppermute | solution.py:382
  142.5 25.4 %collective-permute-start.22 = (bf16[512,384]{1,0:T(8,128)(2,1)S(1)}, bf16[512,384]{1,0:T(8,128)(2,1)}, u32[]{:S(2)}, u32[]{:S(2)}) collective-permute-start(bf16[512,384]{1,0:T(8,128)(2,1)S(1)} %get-tuple-element.104.cp_ref), channel_id=1, source_target_pairs={{0,1},{1,0},{2,3},{3,2},{4,5},{5,4},{6,7},{7,6},{8,9},{9,8},{10,11... | collective-permute-start | bytes 1179656 | tf_op jit(solution)/shard_map/ppermute | solution.py:842
  166.9 24.9 %collective-permute-start.25 = (bf16[512,384]{1,0:T(8,128)(2,1)}, bf16[512,384]{1,0:T(8,128)(2,1)S(1)}, u32[]{:S(2)}, u32[]{:S(2)}) collective-permute-start(bf16[512,384]{1,0:T(8,128)(2,1)} %get-tuple-element.124), channel_id=1, source_target_pairs={{0,1},{1,0},{2,3},{3,2},{4,5},{5,4},{6,7},{7,6},{8,9},{9,8},{10,11... | collective-permute-start | bytes 1179656 | tf_op jit(solution)/shard_map/ppermute | solution.py:842
  190.6 22.7 %collective-permute-start.24 = (bf16[512,384]{1,0:T(8,128)(2,1)}, bf16[512,384]{1,0:T(8,128)(2,1)S(1)}, u32[]{:S(2)}, u32[]{:S(2)}) collective-permute-start(bf16[512,384]{1,0:T(8,128)(2,1)} %get-tuple-element.121), channel_id=1, source_target_pairs={{0,1},{1,0},{2,3},{3,2},{4,5},{5,4},{6,7},{7,6},{8,9},{9,8},{10,11... | collective-permute-start | bytes 1179656 | tf_op jit(solution)/shard_map/ppermute | solution.py:842
  212.4 25.4 %collective-permute-start.26 = (bf16[512,768]{1,0:T(8,128)(2,1)S(1)}, bf16[512,768]{1,0:T(8,128)(2,1)S(1)}, u32[]{:S(2)}, u32[]{:S(2)}) collective-permute-start(bf16[512,768]{1,0:T(8,128)(2,1)S(1)} %convolution_convert_fusion.2), channel_id=1, source_target_pairs={{0,1},{1,0},{2,3},{3,2},{4,5},{5,4},{6,7},{7,6},{8,9},{9,8},{10,11... | collective-permute-start | bytes 2359304 | tf_op jit(solution)/shard_map/ppermute | solution.py:842
  237.8 23.4 %collective-permute-start.30 = (bf16[512,768]{1,0:T(8,128)(2,1)}, bf16[512,768]{1,0:T(8,128)(2,1)}, u32[]{:S(2)}, u32[]{:S(2)}) collective-permute-start(bf16[512,768]{1,0:T(8,128)(2,1)} %convolution_convert_fusion.1), channel_id=1, source_target_pairs={{0,1},{1,0},{2,3},{3,2},{4,5},{5,4},{6,7},{7,6},{8,9},{9,8},{10,11... | collective-permute-start | bytes 2359304 | tf_op jit(solution)/shard_map/ppermute | solution.py:842
  (46 other events, 585.9 us)
where the time goes:
time: 278 us; the launch traced here: 273 us
  Pallas kernels  135 us (49%)
  starting transfers between devices  57.5 us (21%)
  waiting for transfers between devices  53 us (19%)
  local copies, waits for them, and re-layouts  13 us (5%)
  matrix products  9.58 us (3%)
  other arithmetic  3.23 us (1%)
    ppermute x24, starting transfers between devices, flipped(): return lax.ppermute(block, 'seq', [(i, i ^ mask) for i in range(count)])  46.3 us
    ppermute x24, waiting for transfers between devices, flipped(): return lax.ppermute(block, 'seq', [(i, i ^ mask) for i in range(count)])  46.1 us
    pallas_call x2, Pallas kernels, ffn(): pl.pallas_call(functools.partial(ffn_kernel, shards=shards, cuts=cuts, ro...  45.2 us
    pallas_call x2, Pallas kernels, attend_back(): pl.pallas_call(functools.partial(attend_back_kernel, hd=hd, row=row), gri...  39.9 us
    pallas_call x2, Pallas kernels, attend(): pl.pallas_call(functools.partial(attend_kernel, hd=hd, row=row), grid_spe...  29.8 us
    pallas_call x1, Pallas kernels, trained(): pl.pallas_call(functools.partial(trained_kernel, wide=wide), grid_spec=pl...  8.8 us
    ppermute x9, starting transfers between devices, swapped(): return lax.ppermute(block, 'blk', [(0, 1), (1, 0)])  8.24 us
    unnamed x75, local copies, waits for them, and re-layouts  7.01 us
  transfers between devices with their start and end apart: 34, of which 12 were waited for; matrix products, arithmetic and copies ran while one was open for 7% of the time, Pallas kernels for 48%

commit v1 on v0

--- a/solution.py
+++ b/solution.py
@@ -16,7 +16,7 @@
 LN2 = 0.6931471805599453
 LOG2E = 1.4426950408889634
 SEGS = 5
-PARTS = 3
+PARTS = 5
 TILE = 256
 STEP = 128
 
@@ -31,8 +31,12 @@
     return [lane_row(lambda l: l == start + n, wide) for n in range(PARTS)]
 
 def spread(column, rows):
-    top = column.astype(bf16).astype(f32)
-    return (top*rows[0] + (column-top)*rows[1]).astype(bf16)
+    total = 0.0
+    for n, row in enumerate(rows):
+        piece = column if n + 1 == len(rows) else column.astype(bf16).astype(f32)
+        total = total + piece*row
+        column = column - piece
+    return total.astype(bf16)
 
 def cross_ones(wide, hd):
     a = lax.broadcasted_iota(jnp.int32, (wide, wide), 0) < hd
@@ -143,7 +147,7 @@
             for s in range(2):
                 plain = qa_ref[s, rows, :] * (1.0 - parts[s][0]).astype(bf16)
                 m = jnp.max(dot_nt(plain, ka[s]), axis=1, keepdims=True)
-                qa_ref[s, rows, :] = plain - (jnp.broadcast_to(m, (TILE, wide))*parts[s][0]).astype(bf16)
+                qa_ref[s, rows, :] = plain + spread(-jnp.broadcast_to(m, (TILE, wide)), parts[s][:3])
             weigh(rows, slice(0, span))
             return carry
         lax.fori_loop(0, span//TILE, exact_tile, 0)
@@ -151,7 +155,7 @@
     outs[...] = (jnp.where(first, og[0], og[1]) / pltpu.roll(total, hd, 1)).astype(bf16)
     lse = -jnp.log2(total)
     for s in range(2):
-        qa_ref[s] = qa_ref[s] + spread(lse, parts[s][1:])
+        qa_ref[s] = qa_ref[s] + spread(lse, parts[s][3:])
     def leave(n):
         own_ref[...] = outs[n*half:(n+1)*half, :]
         par_ref[...] = outs[(1-n)*half:(2-n)*half, :]
@@ -216,7 +220,7 @@
             for s in range(2):
                 ka[s, rows, :] = kp*sides[s] + kf[s, rows, :]
                 va[s, rows, :] = vp*sides[s] + low[s]
-                ga[s, rows, :] = gp*sides[s] + spread(-delta, parts[s])
+                ga[s, rows, :] = gp*sides[s] + spread(-delta, parts[s][:2])
     by_half(spot[0], place)
     kacc[...] = jnp.zeros_like(kacc)
     vacc[...] = jnp.zeros_like(vacc)

time: 278 us -> 278 us (level)
  Pallas kernels: 135 us -> 161 us
  starting transfers between devices: 57.5 us -> 32 us
    ppermute x24, starting transfers between devices: 46.3 us -> 20.8 us  [flipped(): return lax.ppermute(block, 'seq', [(i, i ^ mask) for i in range(count)])]
    pallas_call x2, Pallas kernels: 29.8 us -> 54.9 us  [attend(): pl.pallas_call(functools.partial(attend_kernel, hd=hd, row=row), grid_spe...]
  transfers between devices with their start and end apart: 34 -> 34, of which waited for: 12 -> 11; matrix products, arithmetic and copies ran while one was open for 7% -> 7% of each run, Pallas kernels for 48% -> 58%
where the time goes in v1:
time: 278 us; the launch traced here: 273 us
  Pallas kernels  161 us (58%)
  waiting for transfers between devices  52.7 us (19%)
  starting transfers between devices  32 us (12%)
  local copies, waits for them, and re-layouts  13.4 us (5%)
  matrix products  9.58 us (3%)
  other arithmetic  3.23 us (1%)
    pallas_call x2, Pallas kernels, attend(): pl.pallas_call(functools.partial(attend_kernel, hd=hd, row=row), grid_spe...  54.9 us
    ppermute x24, waiting for transfers between devices, flipped(): return lax.ppermute(block, 'seq', [(i, i ^ mask) for i in range(count)])  45.8 us
    pallas_call x2, Pallas kernels, ffn(): pl.pallas_call(functools.partial(ffn_kernel, shards=shards, cuts=cuts, ro...  45.2 us
    pallas_call x2, Pallas kernels, attend_back(): pl.pallas_call(functools.partial(attend_back_kernel, hd=hd, row=row), gri...  40.9 us
    ppermute x24, starting transfers between devices, flipped(): return lax.ppermute(block, 'seq', [(i, i ^ mask) for i in range(count)])  20.8 us
    pallas_call x1, Pallas kernels, trained(): pl.pallas_call(functools.partial(trained_kernel, wide=wide), grid_spec=pl...  8.8 us
    ppermute x9, starting transfers between devices, swapped(): return lax.ppermute(block, 'blk', [(0, 1), (1, 0)])  8.19 us
    unnamed x75, local copies, waits for them, and re-layouts  7.39 us
  transfers between devices with their start and end apart: 34, of which 11 were waited for; matrix products, arithmetic and copies ran while one was open for 7% of the time, Pallas kernels for 58%

profile of v1, /device:TPU:0, one launch (start us, length us, event | category | flops | bytes accessed | tf_op | source)
XLA Modules:
  0.0 273.3 jit_solution(13670456746366065693)
XLA Ops:
  1.2 2.9 %shard_map.208 = (bf16[1008,128]{1,0:T(8,128)(2,1)}, bf16[432,768]{1,0:T(8,128)(2,1)}, f32[8,1024]{1,0:T(8,128)}) custom-call(s32[2]{0:T(128)} %pad_add_fusion.place.spot, bf16[48,1024]{1,0:T(8,128)(2,1)} %a_ref.1, bf16[48,768]{1,0:T(8,128)(2,1)} %q_ref.1, bf16[48,768]{1,0:T(8,128)(2,1)} %k_ref.1, bf16[48,768]{1,0:T(8,128)(2,1)} %v_ref.1, ...), custom_call_target="tpu_custom_call" | custom-call | tf_op jit(solution)/shard_map/pallas_call | solution.py:305
  4.1 3.0 %collective-permute-start.3 = (bf16[432,768]{1,0:T(8,128)(2,1)}, bf16[432,768]{1,0:T(8,128)(2,1)S(1)}, u32[]{:S(2)}, u32[]{:S(2)}) collective-permute-start(bf16[432,768]{1,0:T(8,128)(2,1)} %get-tuple-element.93.refs_0_), channel_id=1, source_target_pairs={{0,4},{2,6},{4,0},{6,2},{8,12},{10,14},{12,8},{14,10},{16,20},{18,... | collective-permute-start | bytes 1990664 | tf_op jit(solution)/shard_map/ppermute | solution.py:386
  8.6 3.6 %collective-permute-start.2 = (bf16[1008,128]{1,0:T(8,128)(2,1)}, bf16[1008,128]{1,0:T(8,128)(2,1)S(1)}, u32[]{:S(2)}, u32[]{:S(2)}) collective-permute-start(bf16[1008,128]{1,0:T(8,128)(2,1)} %get-tuple-element.73), channel_id=1, source_target_pairs={{0,24},{2,26},{4,28},{6,30},{8,16},{10,18},{12,20},{14,22},{16,8},... | collective-permute-start | bytes 774152 | tf_op jit(solution)/shard_map/ppermute | solution.py:386
  14.0 5.9 %collective-permute-done.2 = bf16[1008,128]{1,0:T(8,128)(2,1)S(1)} collective-permute-done((bf16[1008,128]{1,0:T(8,128)(2,1)}, bf16[1008,128]{1,0:T(8,128)(2,1)S(1)}, u32[]{:S(2)}, u32[]{:S(2)}) %collective-permute-start.2) | collective-permute-done | bytes 258080 | tf_op jit(solution)/shard_map/ppermute | solution.py:386
  19.9 13.9 %collective-permute-done.1 = bf16[1008,128]{1,0:T(8,128)(2,1)S(1)} collective-permute-done((bf16[1008,128]{1,0:T(8,128)(2,1)}, bf16[1008,128]{1,0:T(8,128)(2,1)S(1)}, u32[]{:S(2)}, u32[]{:S(2)}) %collective-permute-start.1) | collective-permute-done | bytes 258080 | tf_op jit(solution)/shard_map/ppermute | solution.py:386
  34.7 3.0 %collective-permute-start.6 = (bf16[432,768]{1,0:T(8,128)(2,1)}, bf16[432,768]{1,0:T(8,128)(2,1)}, u32[]{:S(2)}, u32[]{:S(2)}) collective-permute-start(bf16[432,768]{1,0:T(8,128)(2,1)} %get-tuple-element.93.refs_0_), channel_id=1, source_target_pairs={{0,16},{1,25},{2,18},{3,27},{4,20},{5,29},{6,22},{7,31},{8,24},{9,... | collective-permute-start | bytes 1990664 | tf_op jit(solution)/shard_map/ppermute | solution.py:392
  37.7 5.5 %collective-permute-done.8 = bf16[2,512,768]{2,1,0:T(8,128)(2,1)S(1)} collective-permute-done((bf16[2,512,768]{2,1,0:T(8,128)(2,1)}, bf16[2,512,768]{2,1,0:T(8,128)(2,1)S(1)}, u32[]{:S(2)}, u32[]{:S(2)}) %collective-permute-start.8) | collective-permute-done | bytes 1572896 | tf_op jit(solution)/shard_map/ppermute | solution.py:846
  45.1 4.8 %copy.27 = bf16[2048,768]{0,1:T(8,128)(2,1)} copy(bf16[2048,768]{1,0:T(8,128)(2,1)} %bitcast.24) | data formatting | bytes 6291456 | tf_op jit(solution)/shard_map/reshape | solution.py:897
  49.9 16.0 %collective-permute-done.7.refs_4_ = bf16[432,768]{1,0:T(8,128)(2,1)} collective-permute-done((bf16[432,768]{1,0:T(8,128)(2,1)}, bf16[432,768]{1,0:T(8,128)(2,1)}, u32[]{:S(2)}, u32[]{:S(2)}) %collective-permute-start.7) | collective-permute-done | bytes 663584 | tf_op jit(solution)/shard_map/ppermute | solution.py:386
  71.1 3.1 %shard_map.209 = (bf16[16,48,1024]{2,1,0:T(8,128)(2,1)S(1)}, bf16[16,64,384]{2,1,0:T(8,128)(2,1)S(1)}, bf16[768,1152]{1,0:T(8,128)(2,1)S(1)}, bf16[768,768]{1,0:T(8,128)(2,1)S(1)}) custom-call(s32[2]{0:T(128)S(1)} %copy-done.3, bf16[4032,128]{1,0:T(8,128)(2,1)S(1)} %constant_dynamic-update-slice_fusion.refs_0_, ...), custom_call_target="tpu_custom_call" | custom-call | flops 12079595520 | bytes 1048576 | tf_op jit(solution)/shard_map/pallas_call | solution.py:364
  76.2 4.6 %convolution_convert_fusion.xo_ref.xp_ref = bf16[2048,1152]{1,0:T(8,128)(2,1)S(1)} fusion(bf16[2048,768]{0,1:T(8,128)(2,1)S(1)} %copy-done.19, bf16[768,1152]{1,0:T(8,128)(2,1)S(1)} %get-tuple-element.83.w_ref), kind=kOutput, calls=%fused_computation | convolution fusion | flops 3626237952 | bytes 9633792 | tf_op jit(solution)/shard_map/dot_general | solution.py:24
  84.1 27.4 %shard_map.210 = (bf16[512,384]{1,0:T(8,128)(2,1)S(1)}, bf16[512,384]{1,0:T(8,128)(2,1)S(1)}, bf16[6,1024,128]{2,1,0:T(8,128)(2,1)S(1)}) custom-call(s32[2]{0:T(128)S(1)} %copy-done.3, s32[2,4]{1,0:T(2,128)S(1)} %copy-done.8, bf16[2048,1152]{1,0:T(8,128)(2,1)S(1)} %convolution_convert_fusion.xo_ref.xp_ref, ...), custom_call_target="tpu_custom_call" | custom-call | flops 6442450944 | bytes 4718592 | tf_op jit(solution)/shard_map/pallas_call | solution.py:168
  114.6 27.5 %shard_map.211 = (bf16[512,384]{1,0:T(8,128)(2,1)S(1)}, bf16[512,384]{1,0:T(8,128)(2,1)S(1)}, bf16[6,1024,128]{2,1,0:T(8,128)(2,1)S(1)}) custom-call(s32[2]{0:T(128)S(1)} %copy-done.3, s32[2,4]{1,0:T(2,128)S(1)} %copy-done.8, bf16[2048,1152]{1,0:T(8,128)(2,1)S(1)} %convolution_convert_fusion.xo_ref.xp_ref, ...), custom_call_target="tpu_custom_call" | custom-call | flops 6442450944 | bytes 4718592 | tf_op jit(solution)/shard_map/pallas_call | solution.py:168
  145.4 22.5 %shard_map.212 = (bf16[2,512,768]{2,1,0:T(8,128)(2,1)}, bf16[2,512,768]{2,1,0:T(8,128)(2,1)}, bf16[512,384]{1,0:T(8,128)(2,1)}, bf16[512,384]{1,0:T(8,128)(2,1)}) custom-call(s32[2]{0:T(128)} %pad_add_fusion.place.spot, bf16[512,384]{1,0:T(8,128)(2,1)} %copy-done.13, bf16[512,384]{1,0:T(8,128)(2,1)} %copy-done.35, bf16[2,512,768]{2,1,0:T(8,128)(2,1)} %x_hbm.3, ...), custom_call_target="tpu_custom_call" | custom-call | flops 43486543872 | bytes 11796480 | tf_op jit(solution)/shard_map/pallas_call | solution.py:593
  168.9 22.7 %shard_map.213 = (bf16[2,512,768]{2,1,0:T(8,128)(2,1)}, bf16[2,512,768]{2,1,0:T(8,128)(2,1)}, bf16[512,384]{1,0:T(8,128)(2,1)}, bf16[512,384]{1,0:T(8,128)(2,1)}) custom-call(s32[2]{0:T(128)} %pad_add_fusion.place.spot, bf16[512,384]{1,0:T(8,128)(2,1)} %copy-done.15, ...), custom_call_target="tpu_custom_call", output_to_operand_aliasing={{0}: (23, {}), {1}: (24, {})} | custom-call | flops 43486543872 | bytes 11796480 | tf_op jit(solution)/shard_map/pallas_call | solution.py:593
  192.8 23.0 %shard_map.214.refs_0_ = bf16[2,1024,1152]{2,1,0:T(8,128)(2,1)} custom-call(s32[2]{0:T(128)S(1)} %copy-done.4, s32[2,4]{1,0:T(2,128)S(1)} %copy-done.8, bf16[2048,1152]{1,0:T(8,128)(2,1)} %copy-done.10, bf16[2048,1152]{1,0:T(8,128)(2,1)} %copy-done.10, bf16[512,384]{1,0:T(8,128)(2,1)S(1)} %copy-done.14, bf16[512,384]{1,0:T(8,128)(2,1)S(1)} %get-tuple-element.99.cp_ref, ...), custom_call_target="tpu_custom_call" | custom-call | flops 16106127360 | bytes 7864320 | tf_op jit(solution)/shard_map/pallas_call | solution.py:250
  215.9 2.6 convolution_convert_fusion.2
  219.5 17.9 %shard_map.215.turned_ref = bf16[2,1024,1152]{2,1,0:T(8,128)(2,1)S(1)} custom-call(s32[2]{0:T(128)S(1)} %copy-done.4, s32[2,4]{1,0:T(2,128)S(1)} %copy-done.8, bf16[2048,1152]{1,0:T(8,128)(2,1)} %copy-done.10, bf16[2048,1152]{1,0:T(8,128)(2,1)} %copy-done.10, bf16[512,384]{1,0:T(8,128)(2,1)S(1)} %copy-done.16, ...), custom_call_target="tpu_custom_call", output_to_operand_aliasing={{}: (9, {})} | custom-call | flops 16106127360 | bytes 7864320 | tf_op jit(solution)/shard_map/pallas_call | solution.py:250
  237.4 2.4 convolution_convert_fusion.1
  240.9 8.8 %shard_map.216 = f32[28,128]{1,0:T(8,128)} custom-call(s32[2]{0:T(128)} %pad_add_fusion.place.spot, bf16[768,2048]{1,0:T(8,128)(2,1)} %bitcast.25, bf16[2048,1152]{1,0:T(8,128)(2,1)} %bitcast.23, f32[8,1024]{1,0:T(8,128)} %get-tuple-element.82.refs_4_.vecs, bf16[768,768]{1,0:T(8,128)(2,1)} %copy-done.11, bf16[16,48,1024]{2,1,0:T(8,128)(2,1)} %copy-done.9, ...), custom_call_target="tpu_custom_call" | custom-call | flops 4831838208 | bytes 12582912 | tf_op jit(solution)/shard_map/pallas_call | solution.py:448
  251.9 2.5 collective-permute-start.28
  257.4 4.6 %collective-permute-start.32 = (f32[28,128]{1,0:T(8,128)S(1)}, f32[28,128]{1,0:T(8,128)S(1)}, u32[]{:S(2)}, u32[]{:S(2)}) collective-permute-start(f32[28,128]{1,0:T(8,128)S(1)} %add.19), channel_id=1, source_target_pairs={{0,24},{2,26},{4,28},{6,30},{8,16},{10,18},{12,20},{14,22},{16,8},... | collective-permute-start | bytes 43016 | tf_op jit(solution)/shard_map/ppermute | solution.py:386
  263.8 2.7 %collective-permute-done.31 = f32[28,128]{1,0:T(8,128)S(1)} collective-permute-done((f32[28,128]{1,0:T(8,128)S(1)}, f32[28,128]{1,0:T(8,128)S(1)}, u32[]{:S(2)}, u32[]{:S(2)}) %collective-permute-start.31) | collective-permute-done | bytes 14368 | tf_op jit(solution)/shard_map/ppermute | solution.py:386
  266.8 5.1 %shard_map.217 = bf16[2,512,768]{2,1,0:T(8,128)(2,1)} custom-call(bf16[2,1024,1152]{2,1,0:T(8,128)(2,1)} %copy-done.1, bf16[768,1152]{1,0:T(8,128)(2,1)S(1)} %get-tuple-element.83.w_ref, bf16[2,512,768]{2,1,0:T(8,128)(2,1)S(1)} %copy-done.2, bf16[512,768]{1,0:T(8,128)(2,1)S(1)} %collective-permute-done.26.refs_0_, ...), custom_call_target="tpu_custom_call" | custom-call | tf_op jit(solution)/shard_map/pallas_call | solution.py:481
  (142 shorter events, 35.9 us)
Async XLA Ops:
  4.1 29.7 %collective-permute-start.3 = (bf16[432,768]{1,0:T(8,128)(2,1)}, bf16[432,768]{1,0:T(8,128)(2,1)S(1)}, u32[]{:S(2)}, u32[]{:S(2)}) collective-permute-start(bf16[432,768]{1,0:T(8,128)(2,1)} %get-tuple-element.93.refs_0_), channel_id=1, source_target_pairs={{0,4},{2,6},{4,0},{6,2},{8,12},{10,14},{12,8},{14,10},{16,20},{18,... | collective-permute-start | bytes 1990664 | tf_op jit(solution)/shard_map/ppermute | solution.py:386
  7.1 36.1 %collective-permute-start.8 = (bf16[2,512,768]{2,1,0:T(8,128)(2,1)}, bf16[2,512,768]{2,1,0:T(8,128)(2,1)S(1)}, u32[]{:S(2)}, u32[]{:S(2)}) collective-permute-start(bf16[2,512,768]{2,1,0:T(8,128)(2,1)} %x_hbm.3), channel_id=1, source_target_pairs={{0,1},{1,0},{2,3},{3,2},{4,5},{5,4},{6,7},{7,6},{8,9},{9,8},{10,11... | collective-permute-start | bytes 4718600 | tf_op jit(solution)/shard_map/ppermute | solution.py:846
  12.2 21.6 %collective-permute-start.1 = (bf16[1008,128]{1,0:T(8,128)(2,1)}, bf16[1008,128]{1,0:T(8,128)(2,1)S(1)}, u32[]{:S(2)}, u32[]{:S(2)}) collective-permute-start(bf16[1008,128]{1,0:T(8,128)(2,1)} %get-tuple-element.73), channel_id=1, source_target_pairs={{0,16},{2,18},{4,20},{6,22},{8,24},{10,26},{12,28},{14,30},{16,0},... | collective-permute-start | bytes 774152 | tf_op jit(solution)/shard_map/ppermute | solution.py:386
  12.2 21.6 %collective-permute-start = (bf16[1008,128]{1,0:T(8,128)(2,1)}, bf16[1008,128]{1,0:T(8,128)(2,1)S(1)}, u32[]{:S(2)}, u32[]{:S(2)}) collective-permute-start(bf16[1008,128]{1,0:T(8,128)(2,1)} %get-tuple-element.73), channel_id=1, source_target_pairs={{0,8},{2,10},{4,12},{6,14},{8,0},{10,2},{12,4},{14,6},{16,24},{18,... | collective-permute-start | bytes 774152 | tf_op jit(solution)/shard_map/ppermute | solution.py:386
  34.0 33.3 %collective-permute-start.5 = (bf16[4032,128]{1,0:T(8,128)(2,1)S(1)}, bf16[4032,128]{1,0:T(8,128)(2,1)S(1)}, u32[]{:S(2)}, u32[]{:S(2)}) collective-permute-start(bf16[4032,128]{1,0:T(8,128)(2,1)S(1)} %constant_dynamic-update-slice_fusion.refs_0_), channel_id=1, source_target_pairs={{0,2},{2,0},{4,6},{6,4},{8,10},{10,8},{12,14},{14,12},{16,18},{18,... | collective-permute-start | bytes 3096584 | tf_op jit(solution)/shard_map/ppermute | solution.py:386
  34.0 33.2 %collective-permute-start.4 = (bf16[4032,128]{1,0:T(8,128)(2,1)S(1)}, bf16[4032,128]{1,0:T(8,128)(2,1)S(1)}, u32[]{:S(2)}, u32[]{:S(2)}) collective-permute-start(bf16[4032,128]{1,0:T(8,128)(2,1)S(1)} %constant_dynamic-update-slice_fusion.refs_0_), channel_id=1, source_target_pairs={{0,4},{2,6},{4,0},{6,2},{8,12},{10,14},{12,8},{14,10},{16,20},{18,... | collective-permute-start | bytes 3096584 | tf_op jit(solution)/shard_map/ppermute | solution.py:386
  34.6 31.3 %collective-permute-start.7 = (bf16[432,768]{1,0:T(8,128)(2,1)}, bf16[432,768]{1,0:T(8,128)(2,1)}, u32[]{:S(2)}, u32[]{:S(2)}) collective-permute-start(bf16[432,768]{1,0:T(8,128)(2,1)} %get-tuple-element.93.refs_0_), channel_id=1, source_target_pairs={{0,8},{2,10},{4,12},{6,14},{8,0},{10,2},{12,4},{14,6},{16,24},{18,... | collective-permute-start | bytes 1990664 | tf_op jit(solution)/shard_map/ppermute | solution.py:386
  34.7 32.5 %collective-permute-start.6 = (bf16[432,768]{1,0:T(8,128)(2,1)}, bf16[432,768]{1,0:T(8,128)(2,1)}, u32[]{:S(2)}, u32[]{:S(2)}) collective-permute-start(bf16[432,768]{1,0:T(8,128)(2,1)} %get-tuple-element.93.refs_0_), channel_id=1, source_target_pairs={{0,16},{1,25},{2,18},{3,27},{4,20},{5,29},{6,22},{7,31},{8,24},{9,... | collective-permute-start | bytes 1990664 | tf_op jit(solution)/shard_map/ppermute | solution.py:392
  68.2 12.6 %collective-permute-start.11 = (bf16[432,768]{1,0:T(8,128)(2,1)}, bf16[432,768]{1,0:T(8,128)(2,1)S(1)}, u32[]{:S(2)}, u32[]{:S(2)}) collective-permute-start(bf16[432,768]{1,0:T(8,128)(2,1)} %collective-permute-done.6.refs_8_), channel_id=1, source_target_pairs={{0,2},{2,0},{4,6},{6,4},{8,10},{10,8},{12,14},{14,12},{16,18},{18,... | collective-permute-start | bytes 1990664 | tf_op jit(solution)/shard_map/ppermute | solution.py:386
  80.8 31.5 %collective-permute-start.13 = (bf16[432,768]{1,0:T(8,128)(2,1)}, bf16[432,768]{1,0:T(8,128)(2,1)S(1)}, u32[]{:S(2)}, u32[]{:S(2)}) collective-permute-start(bf16[432,768]{1,0:T(8,128)(2,1)} %collective-permute-done.6.refs_8_), channel_id=1, source_target_pairs={{0,4},{2,6},{4,0},{6,2},{8,12},{10,14},{12,8},{14,10},{16,20},{18,... | collective-permute-start | bytes 1990664 | tf_op jit(solution)/shard_map/ppermute | solution.py:386
  82.4 30.0 %collective-permute-start.12 = (bf16[432,768]{1,0:T(8,128)(2,1)}, bf16[432,768]{1,0:T(8,128)(2,1)S(1)}, u32[]{:S(2)}, u32[]{:S(2)}) collective-permute-start(bf16[432,768]{1,0:T(8,128)(2,1)} %collective-permute-done.6.refs_8_), channel_id=1, source_target_pairs={{0,1},{1,0},{2,3},{3,2},{4,5},{5,4},{6,7},{7,6},{8,9},{9,8},{10,11... | collective-permute-start | bytes 1990664 | tf_op jit(solution)/shard_map/ppermute | solution.py:846
  82.6 29.7 %collective-permute-start.15 = (bf16[432,768]{1,0:T(8,128)(2,1)S(1)}, bf16[432,768]{1,0:T(8,128)(2,1)S(1)}, u32[]{:S(2)}, u32[]{:S(2)}) collective-permute-start(bf16[432,768]{1,0:T(8,128)(2,1)S(1)} %copy-done.21), channel_id=1, source_target_pairs={{0,2},{2,0},{4,6},{6,4},{8,10},{10,8},{12,14},{14,12},{16,18},{18,... | collective-permute-start | bytes 1990664 | tf_op jit(solution)/shard_map/ppermute | solution.py:386
  82.6 29.7 %collective-permute-start.16 = (bf16[432,768]{1,0:T(8,128)(2,1)S(1)}, bf16[432,768]{1,0:T(8,128)(2,1)S(1)}, u32[]{:S(2)}, u32[]{:S(2)}) collective-permute-start(bf16[432,768]{1,0:T(8,128)(2,1)S(1)} %copy-done.23), channel_id=1, source_target_pairs={{0,2},{2,0},{4,6},{6,4},{8,10},{10,8},{12,14},{14,12},{16,18},{18,... | collective-permute-start | bytes 1990664 | tf_op jit(solution)/shard_map/ppermute | solution.py:386
  83.1 29.2 %collective-permute-start.14 = (bf16[432,768]{1,0:T(8,128)(2,1)S(1)}, bf16[432,768]{1,0:T(8,128)(2,1)S(1)}, u32[]{:S(2)}, u32[]{:S(2)}) collective-permute-start(bf16[432,768]{1,0:T(8,128)(2,1)S(1)} %copy-done.23), channel_id=1, source_target_pairs={{0,8},{2,10},{4,12},{6,14},{8,0},{10,2},{12,4},{14,6},{16,24},{18,... | collective-permute-start | bytes 1990664 | tf_op jit(solution)/shard_map/ppermute | solution.py:386
  112.4 29.7 %collective-permute-start.19 = (bf16[432,768]{1,0:T(8,128)(2,1)S(1)}, bf16[432,768]{1,0:T(8,128)(2,1)S(1)}, u32[]{:S(2)}, u32[]{:S(2)}) collective-permute-start(bf16[432,768]{1,0:T(8,128)(2,1)S(1)} %collective-permute-done.14.refs_6_), channel_id=1, source_target_pairs={{0,2},{2,0},{4,6},{6,4},{8,10},{10,8},{12,14},{14,12},{16,18},{18,... | collective-permute-start | bytes 1990664 | tf_op jit(solution)/shard_map/ppermute | solution.py:386
  112.5 29.7 %collective-permute-start.20 = (bf16[432,768]{1,0:T(8,128)(2,1)S(1)}, bf16[432,768]{1,0:T(8,128)(2,1)S(1)}, u32[]{:S(2)}, u32[]{:S(2)}) collective-permute-start(bf16[432,768]{1,0:T(8,128)(2,1)S(1)} %collective-permute-done.13.refs_10_), channel_id=1, source_target_pairs={{0,2},{2,0},{4,6},{6,4},{8,10},{10,8},{12,14},{14,12},{16,18},{18,... | collective-permute-start | bytes 1990664 | tf_op jit(solution)/shard_map/ppermute | solution.py:386
  113.0 29.2 %collective-permute-start.21 = (bf16[432,768]{1,0:T(8,128)(2,1)S(1)}, bf16[432,768]{1,0:T(8,128)(2,1)S(1)}, u32[]{:S(2)}, u32[]{:S(2)}) collective-permute-start(bf16[432,768]{1,0:T(8,128)(2,1)S(1)} %collective-permute-done.12.refs_12_), channel_id=1, source_target_pairs={{0,2},{2,0},{4,6},{6,4},{8,10},{10,8},{12,14},{14,12},{16,18},{18,... | collective-permute-start | bytes 1990664 | tf_op jit(solution)/shard_map/ppermute | solution.py:386
  113.1 29.1 %collective-permute-start.18 = (bf16[432,768]{1,0:T(8,128)(2,1)S(1)}, bf16[432,768]{1,0:T(8,128)(2,1)S(1)}, u32[]{:S(2)}, u32[]{:S(2)}) collective-permute-start(bf16[432,768]{1,0:T(8,128)(2,1)S(1)} %collective-permute-done.12.refs_12_), channel_id=1, source_target_pairs={{0,4},{2,6},{4,0},{6,2},{8,12},{10,14},{12,8},{14,10},{16,20},{18,... | collective-permute-start | bytes 1990664 | tf_op jit(solution)/shard_map/ppermute | solution.py:386
  113.5 28.6 %collective-permute-start.17 = (bf16[512,384]{1,0:T(8,128)(2,1)S(1)}, bf16[512,384]{1,0:T(8,128)(2,1)S(1)}, u32[]{:S(2)}, u32[]{:S(2)}) collective-permute-start(bf16[512,384]{1,0:T(8,128)(2,1)S(1)} %get-tuple-element.99.cp_ref), channel_id=1, source_target_pairs={{0,1},{1,0},{2,3},{3,2},{4,5},{5,4},{6,7},{7,6},{8,9},{9,8},{10,11... | collective-permute-start | bytes 1179656 | tf_op jit(solution)/shard_map/ppermute | solution.py:846
  143.4 25.5 %collective-permute-start.22 = (bf16[512,384]{1,0:T(8,128)(2,1)S(1)}, bf16[512,384]{1,0:T(8,128)(2,1)}, u32[]{:S(2)}, u32[]{:S(2)}) collective-permute-start(bf16[512,384]{1,0:T(8,128)(2,1)S(1)} %get-tuple-element.104.cp_ref), channel_id=1, source_target_pairs={{0,1},{1,0},{2,3},{3,2},{4,5},{5,4},{6,7},{7,6},{8,9},{9,8},{10,11... | collective-permute-start | bytes 1179656 | tf_op jit(solution)/shard_map/ppermute | solution.py:846
  167.9 24.9 %collective-permute-start.25 = (bf16[512,384]{1,0:T(8,128)(2,1)}, bf16[512,384]{1,0:T(8,128)(2,1)S(1)}, u32[]{:S(2)}, u32[]{:S(2)}) collective-permute-start(bf16[512,384]{1,0:T(8,128)(2,1)} %get-tuple-element.124), channel_id=1, source_target_pairs={{0,1},{1,0},{2,3},{3,2},{4,5},{5,4},{6,7},{7,6},{8,9},{9,8},{10,11... | collective-permute-start | bytes 1179656 | tf_op jit(solution)/shard_map/ppermute | solution.py:846
  191.6 27.9 %collective-permute-start.24 = (bf16[512,384]{1,0:T(8,128)(2,1)}, bf16[512,384]{1,0:T(8,128)(2,1)S(1)}, u32[]{:S(2)}, u32[]{:S(2)}) collective-permute-start(bf16[512,384]{1,0:T(8,128)(2,1)} %get-tuple-element.121), channel_id=1, source_target_pairs={{0,1},{1,0},{2,3},{3,2},{4,5},{5,4},{6,7},{7,6},{8,9},{9,8},{10,11... | collective-permute-start | bytes 1179656 | tf_op jit(solution)/shard_map/ppermute | solution.py:846
  218.5 21.3 %collective-permute-start.26 = (bf16[512,768]{1,0:T(8,128)(2,1)S(1)}, bf16[512,768]{1,0:T(8,128)(2,1)S(1)}, u32[]{:S(2)}, u32[]{:S(2)}) collective-permute-start(bf16[512,768]{1,0:T(8,128)(2,1)S(1)} %convolution_convert_fusion.2), channel_id=1, source_target_pairs={{0,1},{1,0},{2,3},{3,2},{4,5},{5,4},{6,7},{7,6},{8,9},{9,8},{10,11... | collective-permute-start | bytes 2359304 | tf_op jit(solution)/shard_map/ppermute | solution.py:846
  239.8 22.2 %collective-permute-start.30 = (bf16[512,768]{1,0:T(8,128)(2,1)}, bf16[512,768]{1,0:T(8,128)(2,1)}, u32[]{:S(2)}, u32[]{:S(2)}) collective-permute-start(bf16[512,768]{1,0:T(8,128)(2,1)} %convolution_convert_fusion.1), channel_id=1, source_target_pairs={{0,1},{1,0},{2,3},{3,2},{4,5},{5,4},{6,7},{7,6},{8,9},{9,8},{10,11... | collective-permute-start | bytes 2359304 | tf_op jit(solution)/shard_map/ppermute | solution.py:846
  (46 other events, 515.1 us)
